TPU v7x, 512 devices: a whole 4x8x8 slice. The times are simulated.
512 devices in a mesh: dp: 128 (over z, y, core), cent: 4 (over x).
Axes of the slice: x: 4, y: 8, z: 8, core: 2. Of those that a mesh axis runs over, the one named last changes fastest.
Arguments:
- embeddings: float32 [131072, 768], P(('dp', 'cent')), may hold values from -6 to 6
- assignment: int32 [131072, 1], P(('dp', 'cent')), may hold values from 0 to 255; in each aligned block of 256 rows (0 to 255, 256 to 511, ...) at most 2 rows name the same one
- slab_ids: int32 [256], replicated, may hold values from 0 to 65535, as said below
- centroids: float32 [65536, 768], P(('dp', 'cent')), may hold values from -0.21875 to 0.21875
Outputs:
- new_table: float32 [65536, 768], P(('dp', 'cent'))
- centroid_cos: float32 [131072], P(('dp', 'cent'))
- max_sim: float32 [131072], P(('dp', 'cent'))
Inputs may be any that keep to these rules, and one draw needn't show every extreme that they name: `slab_ids`: distinct table rows. `assignment`: among the 256 rows of one device (aligned blocks) no cluster is named by more than 2 rows, a bound that some block reaches; every cluster has at least one row.
All inputs are finite; a program needn't handle non-finite values.
Results may differ from a plain program's by a relative error of at most 0.0003.
Values sent between devices are 32-bit elements; how exact they have to be, the bound alone decides.
A program may use at most 64 MiB of HBM per device.

v0:
```python
import jax
import jax.numpy as jnp
from jax import lax
from jax.sharding import PartitionSpec as P

epsilon = 1e-06


def normalize(values):
    return values * lax.rsqrt(jnp.sum(values * values, axis=-1, keepdims=True) + epsilon)


def cluster_sims(queries, keys):
    return jnp.einsum(
        "cqe,cke->cqk",
        queries,
        keys,
        precision=lax.Precision.HIGHEST,
        preferred_element_type=jnp.float32,
    )


def local(embeddings, assignment, slab_ids, centroids):
    rows, width = embeddings.shape
    slab = slab_ids.shape[0]
    n_dp = lax.axis_size("dp")
    n_cent = lax.axis_size("cent")
    cl_own = slab // n_dp
    cap = 2 * rows // slab
    per_owner = n_dp * cap
    unit = normalize(embeddings)
    labels = assignment[:, 0]
    member = labels[:, None] == jnp.arange(slab, dtype=jnp.int32)[None, :]
    onehot = member.astype(jnp.float32)
    partial_value = lax.dot_general(
        onehot,
        unit,
        (((0,), (0,)), ((), ())),
        precision=lax.Precision.HIGHEST,
        preferred_element_type=jnp.float32,
    )
    totals = lax.psum(partial_value, ("dp", "cent"))
    fresh = normalize(totals)
    table_rows = centroids.shape[0]
    first_row = (lax.axis_index("dp") * n_cent + lax.axis_index("cent")) * table_rows
    global_rows = first_row + jnp.arange(table_rows, dtype=jnp.int32)
    matches = (global_rows[:, None] == slab_ids[None, :]).astype(jnp.float32)
    replaced = jnp.dot(
        matches, fresh, precision=lax.Precision.HIGHEST, preferred_element_type=jnp.float32
    )
    new_table = jnp.where(jnp.sum(matches, axis=1, keepdims=True) > 0.5, replaced, centroids)
    centroid_cos = jnp.sum(unit * jnp.take(fresh, labels, axis=0), axis=1)
    member_int = member.astype(jnp.int32)
    ranks = jnp.sum((jnp.cumsum(member_int, axis=0) - 1) * member_int, axis=1)
    owners = labels // cl_own
    places = labels % cl_own
    target = (places * n_dp + owners) * cap + ranks
    outgoing = jnp.zeros((cl_own * n_dp * cap, width), jnp.float32).at[target].set(unit)
    outgoing = outgoing.reshape(cl_own, n_dp, cap, width)
    present = (
        jnp.zeros((cl_own * n_dp * cap,), jnp.float32)
        .at[target]
        .set(1.0)
        .reshape(cl_own, n_dp, cap)
    )
    arrived, arrived_live = (
        lax.all_to_all(outgoing, "dp", split_axis=1, concat_axis=1, tiled=True),
        lax.all_to_all(present, "dp", split_axis=1, concat_axis=1, tiled=True),
    )
    queries = arrived.reshape(cl_own, per_owner, width)
    query_live = arrived_live.reshape(cl_own, per_owner)
    start_best = jnp.full((cl_own, per_owner), -1.0, jnp.float32)
    query_index = lax.axis_index("cent") * per_owner + jnp.arange(per_owner, dtype=jnp.int32)
    keys = lax.all_gather(queries, "cent", axis=1, tiled=True)
    key_live = lax.all_gather(query_live, "cent", axis=1, tiled=True)
    sims = cluster_sims(queries, keys)
    key_index = jnp.arange(keys.shape[1], dtype=jnp.int32)
    usable = (key_live[:, None, :] > 0.5) & (query_index[:, None] != key_index[None, :])[None, :, :]
    best = jnp.maximum(start_best, jnp.max(jnp.where(usable, sims, -2.0), axis=2))
    answers = lax.all_to_all(
        best.reshape(cl_own, n_dp, cap), "dp", split_axis=1, concat_axis=1, tiled=True
    )
    max_sim = jnp.take(answers.reshape(cl_own * n_dp * cap), target)
    return (new_table, centroid_cos, max_sim)


def solution(mesh):
    placed = (P(("dp", "cent"), None), P(("dp", "cent"), None), P(), P(("dp", "cent"), None))
    return jax.shard_map(
        local,
        mesh=mesh,
        in_specs=placed,
        out_specs=(P(("dp", "cent"), None), P(("dp", "cent")), P(("dp", "cent"))),
        check_vma=False,
    )
```

profile of v0, /device:TPU:1, one launch (start us, length us, event | category | flops | bytes accessed | tf_op | source)
XLA Modules:
  0.0 395.0 jit_solution(5590207578965927314)
XLA Ops:
  8.0 0.0 copy-start.3
  8.0 0.0 copy-start.1
  8.0 0.9 copy.25
  8.9 0.2 fusion.7
  9.1 0.1 add_add_fusion
  9.3 0.9 fusion.8
  10.1 0.0 copy-done.3
  10.2 0.0 copy-done.1
  10.2 0.1 multiply_reduce_fusion.2
  10.3 2.7 scatter_custom_fusion.1
  13.1 2.2 reshape.102
  15.3 1.7 copy.29
  17.0 18.4 %all-to-all-start.1 = ((f32[2,128,2,768]{3,2,0,1:T(2,128)}), f32[2,128,2,768]{3,2,0,1:T(2,128)S(1)}, u32[]{:S(2)}, u32[]{:S(2)}) async-start(f32[2,128,2,768]{3,2,0,1:T(2,128)} %copy.29), calls=%async_computation.1 | async-start | bytes 3145728 | tf_op jit(solution)/shard_map/all_to_all | solution.py:67
  35.4 0.0 all-reduce.2.cloned.1.call-start
  35.5 1.7 fusion.3
  37.2 0.0 all-reduce.2.cloned.1.call-update
  37.2 0.0 all-gather.2.cloned.1.call-start
  37.2 39.9 %all-to-all-done.1 = f32[2,128,2,768]{3,2,0,1:T(2,128)S(1)} async-done(((f32[2,128,2,768]{3,2,0,1:T(2,128)}), f32[2,128,2,768]{3,2,0,1:T(2,128)S(1)}, u32[]{:S(2)}, u32[]{:S(2)}) %all-to-all-start.1) | async-done | bytes 1572896 | tf_op jit(solution)/shard_map/all_to_all | solution.py:67
  77.1 1.7 copy.30
  78.8 3.1 reshape.103
  81.9 0.0 copy-start.4
  81.9 0.0 all-gather.2.cloned.1.call-update
  82.0 1.4 scatter_custom_fusion
  83.4 0.1 reshape.100
  83.5 0.8 copy.27
  84.3 7.3 %all-to-all-start = ((f32[2,128,2]{2,0,1:T(2,128)}), f32[2,128,2]{2,0,1:T(2,128)S(1)}, u32[]{:S(2)}, u32[]{:S(2)}) async-start(f32[2,128,2]{2,0,1:T(2,128)} %copy.27), calls=%async_computation | async-start | bytes 262144 | tf_op jit(solution)/shard_map/all_to_all | solution.py:68
  91.6 0.0 copy-done.4
  91.6 0.2 fusion.11
  91.8 0.2 iota_compare_fusion
  92.0 12.6 %all-to-all-done = f32[2,128,2]{2,0,1:T(2,128)S(1)} async-done(((f32[2,128,2]{2,0,1:T(2,128)}), f32[2,128,2]{2,0,1:T(2,128)S(1)}, u32[]{:S(2)}, u32[]{:S(2)}) %all-to-all-start) | async-done | bytes 2080 | tf_op jit(solution)/shard_map/all_to_all | solution.py:68
  104.6 0.1 reshape.101
  104.8 9.7 %all_gather.6 = f32[2,1024]{1,0:T(2,128)S(1)} all-gather(f32[2,256]{1,0:T(2,128)S(1)} %reshape.101), channel_id=1, replica_groups=mesh['dp'=128,'cent'=4] {'cent'}, dimensions={1}, use_global_device_ids=true | all-gather | bytes 10240 | tf_op jit(solution)/shard_map/all_gather | solution.py:75
  114.5 232.8 %all-reduce.2.cloned.1.call-done = f32[256,768]{1,0:T(8,128)} async-done(((f32[256,768]{1,0:T(8,128)}), f32[256,768]{1,0:T(8,128)}) %all-reduce.2.cloned.1.call-update) | async-done | bytes 786448 | tf_op jit(solution)/shard_map/psum | solution.py:42
  347.2 1.3 multiply_reduce_fusion.1
  348.5 1.3 broadcast_multiply_fusion
  349.8 2.0 gather_fusion
  351.8 2.3 convolution_select_fusion
  354.1 0.0 copy-done
  354.1 7.8 %select_reduce_fusion = f32[2,256]{1,0:T(2,128)S(1)} fusion(f32[2,256,768]{2,1,0:T(8,128)S(1)} %copy-done, f32[2,1024,768]{2,1,0:T(8,128)} %all-gather.2.cloned.1.call-done, pred[256,1024]{1,0:T(8,128)(4,1)S(1)} %iota_compare_fusion, pred[2,1024]{1,0:T(4,128)(4,1)S(1)} %broadcast_compare_fusion), kind=kOutput, calls=%fused_computation.4 | convolution fusion | flops 4833410560 | bytes 8130560 | tf_op jit(solution)/shard_map/cqe,cke->cqk/dot_general | solution.py:14
  361.9 0.1 max_broadcast_in_dim.8
  362.1 0.7 copy.31
  362.8 9.4 %all-to-all-start.2 = ((f32[2,128,2]{2,0,1:T(2,128)}), f32[2,128,2]{2,0,1:T(2,128)S(1)}, u32[]{:S(2)}, u32[]{:S(2)}) async-start(f32[2,128,2]{2,0,1:T(2,128)} %copy.31), calls=%async_computation.2 | async-start | bytes 262144 | tf_op jit(solution)/shard_map/all_to_all | solution.py:80
  372.2 0.0 copy-done.2
  372.2 0.8 multiply_reduce_fusion
  373.0 11.9 %all-to-all-done.2 = f32[2,128,2]{2,0,1:T(2,128)S(1)} async-done(((f32[2,128,2]{2,0,1:T(2,128)}), f32[2,128,2]{2,0,1:T(2,128)S(1)}, u32[]{:S(2)}, u32[]{:S(2)}) %all-to-all-start.2) | async-done | bytes 2080 | tf_op jit(solution)/shard_map/all_to_all | solution.py:80
  384.9 0.1 reshape.104
  385.1 1.9 gather_fusion.1
  387.0 0.6 broadcast_select_fusion
  (20 shorter events, 0.2 us)
Async XLA Ops:
  8.0 2.2 copy-start.3
  8.0 2.2 copy-start.1
  17.0 60.1 %all-to-all-start.1 = ((f32[2,128,2,768]{3,2,0,1:T(2,128)}), f32[2,128,2,768]{3,2,0,1:T(2,128)S(1)}, u32[]{:S(2)}, u32[]{:S(2)}) async-start(f32[2,128,2,768]{3,2,0,1:T(2,128)} %copy.29), calls=%async_computation.1 | async-start | bytes 3145728 | tf_op jit(solution)/shard_map/all_to_all | solution.py:67
  35.4 311.8 %all-reduce.2.cloned.1.call-start = ((), (), s32[]{:S(2)}) async-start(), calls=%async_computation.3 | async-start | bytes 1572864 | tf_op jit(solution)/shard_map/psum | solution.py:42
  37.2 316.9 %all-gather.2.cloned.1.call-start = ((), (), s32[]{:S(2)}) async-start(), calls=%async_computation.4 | async-start | bytes 7864320 | tf_op jit(solution)/shard_map/all_gather | solution.py:74
  81.9 9.7 %copy-start.4 = (s32[256]{0:T(256)S(1)}, s32[256]{0:T(256)}, u32[]{:S(2)}) copy-start(s32[256]{0:T(256)} %param.6) | copy-start | bytes 3076
  84.3 20.3 %all-to-all-start = ((f32[2,128,2]{2,0,1:T(2,128)}), f32[2,128,2]{2,0,1:T(2,128)S(1)}, u32[]{:S(2)}, u32[]{:S(2)}) async-start(f32[2,128,2]{2,0,1:T(2,128)} %copy.27), calls=%async_computation | async-start | bytes 262144 | tf_op jit(solution)/shard_map/all_to_all | solution.py:68
  351.8 2.3 copy-start
  354.1 18.1 %copy-start.2 = (f32[256,768]{1,0:T(8,128)S(1)}, f32[256,768]{1,0:T(8,128)}, u32[]{:S(2)}) copy-start(f32[256,768]{1,0:T(8,128)} %gather_fusion) | copy-start | bytes 2359300
  362.8 22.1 %all-to-all-start.2 = ((f32[2,128,2]{2,0,1:T(2,128)}), f32[2,128,2]{2,0,1:T(2,128)S(1)}, u32[]{:S(2)}, u32[]{:S(2)}) async-start(f32[2,128,2]{2,0,1:T(2,128)} %copy.31), calls=%async_computation.2 | async-start | bytes 262144 | tf_op jit(solution)/shard_map/all_to_all | solution.py:80
Sparse Core Ops, SparseCore 0:
  41.3 305.8 all-reduce.1
Sparse Core Ops, SparseCore 1:
  82.0 65.7 all-gather.1
where the time goes:
time: 396 us; the launch traced here: 395 us
  waiting for transfers between devices  297 us (75%)
  starting transfers between devices  35.2 us (9%)
  local copies, waits for them, and re-layouts  17.1 us (4%)
  between operations  15.7 us (4%)
  matrix products  11.8 us (3%)
  blocking collectives  9.66 us (2%)
  other arithmetic  8.48 us (2%)
    psum x1, waiting for transfers between devices, local(): totals = lax.psum(partial_value, ('dp', 'cent'))  233 us
    all_to_all x1, waiting for transfers between devices, local(): lax.all_to_all(outgoing, 'dp', split_axis=1, concat_axis=1, tiled=True)  39.9 us
    all_to_all x1, starting transfers between devices, local(): lax.all_to_all(outgoing, 'dp', split_axis=1, concat_axis=1, tiled=True)  18.4 us
    all_to_all x1, waiting for transfers between devices, local(): lax.all_to_all(present, 'dp', split_axis=1, concat_axis=1, tiled=True)  12.6 us
    all_to_all x1, waiting for transfers between devices, local(): lax.all_to_all(best.reshape(cl_own, n_dp, cap), 'dp', split_axis=1, conca...  11.9 us
    all_gather x1, blocking collectives, local(): key_live = lax.all_gather(query_live, 'cent', axis=1, tiled=True)  9.66 us
    all_to_all x1, starting transfers between devices, local(): lax.all_to_all(best.reshape(cl_own, n_dp, cap), 'dp', split_axis=1, conca...  9.4 us
  transfers between devices with their start and end apart: 5, of which 4 were waited for; matrix products, arithmetic and copies ran while one was open for 4% of the time, Pallas kernels for 0%

commit v1 on v0

v1 whole, which is shorter than its diff:
```python
import functools

import jax
import jax.numpy as jnp
from jax import lax
from jax.experimental import pallas as pl
from jax.experimental.pallas import tpu as pltpu
from jax.sharding import PartitionSpec as P

epsilon = 1e-06
Z, Y, X = 8, 8, 4
GROUP = 8
SENTINEL = 4.0
MESH = pl.DeviceIdType.MESH
f32, bf16 = jnp.float32, jnp.bfloat16


def split3(v):
    hi = v.astype(bf16)
    rest = v - hi.astype(f32)
    mid = rest.astype(bf16)
    lo = (rest - mid.astype(f32)).astype(bf16)
    return hi, mid, lo


def select_rows(onehot, v):
    hi, mid, lo = split3(v)
    dot = functools.partial(jnp.dot, preferred_element_type=f32)
    return dot(onehot, hi) + dot(onehot, mid) + dot(onehot, lo)


def dot_nt(a, b):
    return lax.dot_general(a, b, (((1,), (1,)), ((), ())), preferred_element_type=f32)


def iota(shape, axis):
    return lax.broadcasted_iota(jnp.int32, shape, axis)


def kernel(dims, emb, lab, slab, cent, table, cos_out, sim_out,
           send, recv, other, khi, klo, bias, frow, fpart, abuf, ans,
           line_sem, plane_sem, own_sem,
           fs, fr, ps, pr, ns, nr, xs_, xr, cs, cr, as_, ar, bs, br):
    Z, Y, X = dims
    nyz = Z * Y
    chips = nyz * X
    n_group = nyz // GROUP
    rows, width = emb.shape
    tiles = width // 128
    half_t = tiles // 2
    msg = 2 * tiles
    own = 2 * chips

    dp = lax.axis_index("dp")
    x = lax.axis_index("cent")
    core = dp % 2
    yz = dp // 2
    y = yz % Y
    z = yz // Y
    me = x * nyz + yz

    def device(zz, yy, xx, cc):
        return ((zz * Y + yy) * 2 + cc, xx)

    barrier = pltpu.get_barrier_semaphore()

    def signal(sem, zz, yy, xx, cc):
        pl.semaphore_signal(sem, inc=1, device_id=device(zz, yy, xx, cc), device_id_type=MESH)

    for d in range(1, Z):
        signal(barrier, (z + d) % Z, y, x, core)
    for d in range(1, Y):
        signal(barrier, z, (y + d) % Y, x, core)
    for d in range(1, X):
        signal(barrier, z, y, (x + d) % X, core)
    signal(barrier, z, y, x, 1 - core)

    e = emb[...]
    unit = e * lax.rsqrt(jnp.sum(e * e, axis=1, keepdims=True) + epsilon)

    pl.semaphore_wait(barrier, Z + Y + X - 2)
    for d in range(1, Y):
        signal(line_sem, z, (y + d) % Y, x, core)

    lrow = lab[...]
    lcol = jnp.broadcast_to(lrow.astype(f32), (128, rows)).T[:, 0:1].astype(jnp.int32)
    earlier = (lcol == lrow) & (iota((rows, rows), 0) < iota((rows, rows), 1))
    rank = jnp.sum(jnp.where(earlier, 1.0, 0.0), axis=0, keepdims=True).astype(jnp.int32)
    target = 2 * lrow + rank
    place = jnp.where(iota((own, rows), 0) == target, 1.0, 0.0)
    filled = jnp.sum(place, axis=1, keepdims=True) > 0.5
    slots = select_rows(place.astype(bf16), unit)
    slots = jnp.where(filled, slots, SENTINEL)
    for t in range(tiles):
        send[pl.ds(t, own, stride=tiles), :] = slots[:, t * 128:(t + 1) * 128]

    pl.semaphore_wait(line_sem, Y - 1)
    for d in range(1, X):
        signal(plane_sem, z, y, (x + d) % X, core)
    pl.semaphore_wait(plane_sem, X - 1)

    def offset(q):
        w = (q * 37) % nyz
        return w // Y, w % Y

    def forward(q, dx, g):
        dz, dy = offset(q)
        zz, yy, xx = (z + dz) % Z, (y + dy) % Y, (x + dx) % X
        c = xx * nyz + zz * Y + yy
        pltpu.make_async_remote_copy(
            src_ref=send.at[pl.ds(c * msg, msg)],
            dst_ref=recv.at[pl.ds((q * X + dx) * msg, msg)],
            send_sem=fs, recv_sem=fr.at[g],
            device_id=device(zz, yy, xx, core), device_id_type=MESH,
        ).start()

    own_copy = pltpu.make_async_copy(
        send.at[pl.ds(me * msg, msg)], recv.at[pl.ds(0, msg)], own_sem)
    own_copy.start()
    for dx in range(1, X):
        forward(0, dx, 0)

    def forward_step(q, carry):
        for dx in range(X):
            forward(q, dx, q // GROUP)
        return carry

    lax.fori_loop(1, nyz, forward_step, 0)
    own_copy.wait()

    grows = GROUP * X * msg
    krows = GROUP * X * 2

    def wait_rows(buf, start, count, sem):
        part = buf.at[pl.ds(start, count)]
        pltpu.make_async_copy(part, part, sem).wait()

    def take(buf, g, base, total):
        columns = []
        dead = None
        for t in range(tiles):
            parts = []
            for dx in range(X):
                for s in range(2):
                    start = g * grows + dx * msg + s * tiles + t
                    parts.append(buf[pl.ds(start, GROUP, stride=X * msg), :])
            v = jnp.concatenate(parts, axis=0)
            if dead is None:
                dead = v > 2.0
                bias[pl.ds(base + g * krows, krows), :] = jnp.where(dead, -4.0, 0.0)
            v = jnp.where(dead, 0.0, v)
            hi = v.astype(bf16)
            lo = (v - hi.astype(f32)).astype(bf16)
            khi[pl.ds(base + g * krows, krows), t * 128:(t + 1) * 128] = hi
            klo[pl.ds(base + g * krows, krows), t * 128:(t + 1) * 128] = lo
            columns.append(jnp.sum(v, axis=0, keepdims=True))
        return total + jnp.concatenate(columns, axis=1)

    mine = jnp.zeros((1, width), f32)
    theirs = jnp.zeros((1, width), f32)
    for g in range(n_group):
        missing = msg if g == 0 else 0
        wait_rows(recv, g * grows + missing, grows - missing, fr.at[g])
        pltpu.make_async_remote_copy(
            src_ref=recv.at[pl.ds(g * grows, grows)],
            dst_ref=other.at[pl.ds(g * grows, grows)],
            send_sem=ps, recv_sem=pr.at[g],
            device_id=device(z, y, x, 1 - core), device_id_type=MESH,
        ).start()
        mine = take(recv, g, 0, mine)
        if g > 0:
            wait_rows(other, (g - 1) * grows, grows, pr.at[g - 1])
            theirs = take(other, g - 1, own, theirs)
    wait_rows(other, (n_group - 1) * grows, grows, pr.at[n_group - 1])
    theirs = take(other, n_group - 1, own, theirs)

    sums = mine + theirs
    fresh = sums * lax.rsqrt(jnp.sum(sums * sums, axis=1, keepdims=True) + epsilon)
    for t in range(half_t):
        a = fresh[:, t * 128:(t + 1) * 128]
        b = fresh[:, (half_t + t) * 128:(half_t + t + 1) * 128]
        frow[pl.ds(me * half_t + t, 1), :] = jnp.where(core == 0, a, b)

    def fresh_step(q, carry):
        dz, dy = offset(q)
        part = frow.at[pl.ds(me * half_t, half_t)]
        pltpu.make_async_remote_copy(
            src_ref=part, dst_ref=part, send_sem=ns, recv_sem=nr,
            device_id=device((z + dz) % Z, (y + dy) % Y, x, core), device_id_type=MESH,
        ).start()
        return carry

    lax.fori_loop(1, nyz, fresh_step, 0)

    qh = khi[0:own, :]
    ql = klo[0:own, :]
    block = own // 2

    def sims(kb, best):
        kh = khi[kb * block:(kb + 1) * block, :]
        kl = klo[kb * block:(kb + 1) * block, :]
        s = dot_nt(kh, qh) + dot_nt(kh, ql) + dot_nt(kl, qh)
        off = bias[kb * block:(kb + 1) * block, :]
        s = s + (jnp.concatenate([off] * (own // 128), axis=1) if own > 128 else off[:, :own])
        if kb < 2:
            itself = iota((block, own), 0) + kb * block == iota((block, own), 1)
            s = jnp.where(itself, -4.0, s)
        return jnp.maximum(best, jnp.max(s, axis=0, keepdims=True))

    best = jnp.full((1, own), -1.0, f32)
    best = sims(0, best)
    best = sims(1, best)

    xrows = nyz * half_t
    wait_rows(frow, 0, (nyz - 1) * half_t, nr)

    def pass_on(dx):
        part = pl.ds(((x + X - dx) % X) * xrows, xrows)
        pltpu.make_async_remote_copy(
            src_ref=frow.at[part], dst_ref=fpart.at[part], send_sem=cs, recv_sem=cr.at[dx],
            device_id=device(z, y, x, 1 - core), device_id_type=MESH,
        ).start()

    for dx in range(1, X):
        part = frow.at[pl.ds(x * xrows, xrows)]
        pltpu.make_async_remote_copy(
            src_ref=part, dst_ref=part, send_sem=xs_, recv_sem=xr.at[dx],
            device_id=device(z, y, (x + dx) % X, core), device_id_type=MESH,
        ).start()
    pass_on(0)

    best = sims(2, best)
    best = sims(3, best)

    fh = fresh.astype(bf16)
    fl = jnp.broadcast_to(fresh - fh.astype(f32), (16, width)).astype(bf16)
    fh = jnp.broadcast_to(fresh, (16, width)).astype(bf16)
    cos = (dot_nt(fh, qh) + dot_nt(fh, ql) + dot_nt(fl, qh))[0:1, :]

    lane_of = 2 * ((iota((128, own), 1) // GROUP) % (2 * X))
    j = iota((128, own), 0)
    spread = jnp.where(j == lane_of, best, jnp.where(j == lane_of + 1, cos, 0.0))
    spread = spread.T.reshape(n_group, 2 * X, GROUP, 128)
    abuf[...] = jnp.sum(spread, axis=1).reshape(nyz, 128)
    ans[pl.ds(me, 1), :] = abuf[0:1, :]

    def answer_step(q, carry):
        dz, dy = offset(q)
        pltpu.make_async_remote_copy(
            src_ref=abuf.at[pl.ds(q, 1)], dst_ref=ans.at[pl.ds(me, 1)],
            send_sem=as_, recv_sem=ar,
            device_id=device((z + Z - dz) % Z, (y + Y - dy) % Y, x, core), device_id_type=MESH,
        ).start()
        return carry

    lax.fori_loop(1, nyz, answer_step, 0)

    for dx in range(1, X):
        wait_rows(frow, ((x + X - dx) % X) * xrows, xrows, xr.at[dx])
        pass_on(dx)

    wait_rows(ans, 0, nyz - 1, ar)
    for dx in range(1, X):
        part = ans.at[pl.ds(x * nyz, nyz)]
        pltpu.make_async_remote_copy(
            src_ref=part, dst_ref=part, send_sem=bs, recv_sem=br.at[dx],
            device_id=device(z, y, (x + dx) % X, core), device_id_type=MESH,
        ).start()

    for dx in range(X):
        wait_rows(fpart, ((x + X - dx) % X) * xrows, xrows, cr.at[dx])
    low, high = [], []
    for t in range(half_t):
        a = frow[pl.ds(t, chips, stride=half_t), :]
        b = fpart[pl.ds(t, chips, stride=half_t), :]
        low.append(jnp.where(core == 0, a, b))
        high.append(jnp.where(core == 0, b, a))
    full = jnp.concatenate(low + high, axis=1)
    trows = cent.shape[0]
    row_id = (dp * X + x) * trows + iota((trows, chips), 0)
    hit = jnp.where(row_id == slab[...], 1.0, 0.0)
    named = jnp.sum(hit, axis=1, keepdims=True) > 0.5
    table[...] = jnp.where(named, select_rows(hit.astype(bf16), full), cent[...])

    for dx in range(1, X):
        wait_rows(ans, ((x + X - dx) % X) * nyz, nyz, br.at[dx])
    member = iota((chips, rows), 0) == lrow
    first = member & (rank == 0)
    second = member & (rank == 1)
    got = ans[...]
    dx_of = (iota((chips, 128), 0) // nyz + X - x) % X
    lane = iota((chips, 128), 1) - 4 * dx_of

    def pick(v):
        a = jnp.sum(jnp.where(lane == v, got, 0.0), axis=1, keepdims=True)
        b = jnp.sum(jnp.where(lane == 2 + v, got, 0.0), axis=1, keepdims=True)
        return jnp.sum(jnp.where(first, a, jnp.where(second, b, 0.0)), axis=0, keepdims=True)

    sim_out[...] = pick(0)
    cos_out[...] = pick(1)

    wait_rows(send, 0, (chips - 1) * msg, fs)
    wait_rows(recv, 0, n_group * grows, ps)
    wait_rows(frow, 0, (nyz - 1) * half_t, ns)
    wait_rows(frow, 0, (X - 1) * xrows, xs_)
    wait_rows(frow, 0, X * xrows, cs)
    wait_rows(ans, 0, nyz - 1, as_)
    wait_rows(ans, 0, (X - 1) * nyz, bs)


def local(dims, embeddings, assignment, slab_ids, centroids):
    Z, Y, X = dims
    nyz = Z * Y
    chips = nyz * X
    rows, width = embeddings.shape
    tiles = width // 128
    n_group = nyz // GROUP
    linear = 2 * chips * tiles
    dma = pltpu.SemaphoreType.DMA
    vmem = pl.BlockSpec(memory_space=pltpu.VMEM)
    table, cos, sim = pl.pallas_call(
        functools.partial(kernel, dims),
        out_shape=(
            jax.ShapeDtypeStruct(centroids.shape, f32),
            jax.ShapeDtypeStruct((1, rows), f32),
            jax.ShapeDtypeStruct((1, rows), f32),
        ),
        in_specs=[vmem] * 4,
        out_specs=(vmem,) * 3,
        scratch_shapes=[
            pltpu.VMEM((linear, 128), f32),
            pltpu.VMEM((linear, 128), f32),
            pltpu.VMEM((linear, 128), f32),
            pltpu.VMEM((4 * chips, width), bf16),
            pltpu.VMEM((4 * chips, width), bf16),
            pltpu.VMEM((4 * chips, 128), f32),
            pltpu.VMEM((chips * tiles // 2, 128), f32),
            pltpu.VMEM((chips * tiles // 2, 128), f32),
            pltpu.VMEM((nyz, 128), f32),
            pltpu.VMEM((chips, 128), f32),
            pltpu.SemaphoreType.REGULAR,
            pltpu.SemaphoreType.REGULAR,
            dma,
            dma, dma((n_group,)), dma, dma((n_group,)),
            dma, dma, dma, dma((X,)), dma, dma((X,)),
            dma, dma, dma, dma((X,)),
        ],
        compiler_params=pltpu.CompilerParams(
            collective_id=0, has_side_effects=True, vmem_limit_bytes=40 * 2**20
        ),
    )(embeddings, assignment.reshape(1, rows), slab_ids.reshape(1, chips), centroids)
    return table, cos.reshape(rows), sim.reshape(rows)


def solution(mesh, dims=(Z, Y, X)):
    placed = (P(("dp", "cent"), None), P(("dp", "cent"), None), P(), P(("dp", "cent"), None))
    return jax.shard_map(
        functools.partial(local, dims),
        mesh=mesh,
        in_specs=placed,
        out_specs=(P(("dp", "cent"), None), P(("dp", "cent")), P(("dp", "cent"))),
        check_vma=False,
    )
```

time: 396 us -> 86.9 us (0.22)
  waiting for transfers between devices: 297 us -> 0 us
  Pallas kernels: 0 us -> 81.3 us
  starting transfers between devices: 35.2 us -> 0 us
  between operations: 15.7 us -> 0.66 us
  local copies, waits for them, and re-layouts: 17.1 us -> 4.68 us
  matrix products: 11.8 us -> 0 us
  blocking collectives: 9.66 us -> 0 us
  other arithmetic: 8.48 us -> 0 us
    psum x1 -> x0, waiting for transfers between devices: 233 us -> none  [local(): totals = lax.psum(partial_value, ('dp', 'cent'))]
    pallas_call x0 -> x1, Pallas kernels: none -> 81.3 us  [local(): pl.pallas_call(functools.partial(kernel, dims), out_shape=(jax.ShapeDtype...]
    all_to_all x3 -> x0, waiting for transfers between devices: 64.4 us -> none  [the longest x1 39.9 us: local(): lax.all_to_all(outgoing, 'dp', split_axis=1, concat_axis=1, tiled=True)]
    all_to_all x3 -> x0, starting transfers between devices: 35.1 us -> none  [the longest x1 18.4 us: local(): lax.all_to_all(outgoing, 'dp', split_axis=1, concat_axis=1, tiled=True)]
    dot_general x3 -> x0, matrix products: 11.8 us -> none  [the longest x1 7.82 us: cluster_sims(): jnp.einsum('cqe,cke->cqk', queries, keys, precision=lax.Precision.HIGHEST...]
    all_gather x1 -> x0, blocking collectives: 9.66 us -> none  [local(): key_live = lax.all_gather(query_live, 'cent', axis=1, tiled=True)]
    reshape x7 -> x0, local copies, waits for them, and re-layouts: 8.22 us -> none  [the longest x2 3.92 us: local(): outgoing = outgoing.reshape(cl_own, n_dp, cap, width)]
    unnamed x10 -> x11, local copies, waits for them, and re-layouts: 0.02 us -> 4.68 us
  transfers between devices with their start and end apart: 5 -> 0, of which waited for: 4 -> 0; matrix products, arithmetic and copies ran while one was open for 4% -> 0% of each run, Pallas kernels for 0% -> 0%
where the time goes in v1:
time: 86.9 us; the launch traced here: 86.6 us
  Pallas kernels  81.3 us (94%)
  local copies, waits for them, and re-layouts  4.68 us (5%)
    pallas_call x1, Pallas kernels, local(): pl.pallas_call(functools.partial(kernel, dims), out_shape=(jax.ShapeDtype...  81.3 us
    unnamed x11, local copies, waits for them, and re-layouts  4.68 us

profile of v1, /device:TPU:1, one launch (start us, length us, event | category | flops | bytes accessed | tf_op | source)
XLA Modules:
  0.0 86.6 jit_solution(9198667055001973346)
XLA Ops:
  0.6 0.0 copy-start.3
  0.6 0.0 copy-start.2
  0.7 0.7 copy-done.3
  1.3 0.0 copy-done.2
  1.3 0.0 copy-start
  1.3 1.1 %copy-done = f32[256,768]{1,0:T(8,128)S(1)} copy-done((f32[256,768]{1,0:T(8,128)S(1)}, f32[256,768]{1,0:T(8,128)}, u32[]{:S(2)}) %copy-start) | copy-done | bytes 786456
  2.5 0.0 copy-start.1
  2.5 1.0 %copy-done.1 = f32[128,768]{1,0:T(8,128)S(1)} copy-done((f32[128,768]{1,0:T(8,128)S(1)}, f32[128,768]{1,0:T(8,128)}, u32[]{:S(2)}) %copy-start.1) | copy-done | bytes 393240
  3.5 81.3 %shard_map.67 = (f32[128,768]{1,0:T(8,128)S(1)}, f32[1,256]{1,0:T(1,128)S(1)}, f32[1,256]{1,0:T(1,128)S(1)}) custom-call(f32[256,768]{1,0:T(8,128)S(1)} %copy-done, s32[1,256]{1,0:T(1,128)S(1)} %bitcast.4, s32[1,256]{1,0:T(1,128)S(1)} %bitcast.5, f32[128,768]{1,0:T(8,128)S(1)} %copy-done.1), custom_call_target="tpu_custom_call" | custom-call | tf_op jit(solution)/shard_map/pallas_call | solution.py:321
  84.8 0.7 copy.10
  85.5 0.6 copy.11
  86.1 0.6 copy.12
Async XLA Ops:
  0.6 0.7 copy-start.3
  0.6 0.7 copy-start.2
  1.3 1.1 %copy-start = (f32[256,768]{1,0:T(8,128)S(1)}, f32[256,768]{1,0:T(8,128)}, u32[]{:S(2)}) copy-start(f32[256,768]{1,0:T(8,128)} %emb.1) | copy-start | bytes 2359300
  2.5 1.0 %copy-start.1 = (f32[128,768]{1,0:T(8,128)S(1)}, f32[128,768]{1,0:T(8,128)}, u32[]{:S(2)}) copy-start(f32[128,768]{1,0:T(8,128)} %cent.1) | copy-start | bytes 1179652

commit v2 on v1

--- a/solution.py
+++ b/solution.py
@@ -33,13 +33,35 @@
     return lax.dot_general(a, b, (((1,), (1,)), ((), ())), preferred_element_type=f32)
 
 
+def yz_offsets(Z, Y):
+    seen, runs = {(0, 0)}, []
+    for dz in range(Z):
+        for dy in range(Y):
+            run, a, b = [], dz, dy
+            for _ in range(4):
+                if (a, b) not in seen:
+                    seen.add((a, b))
+                    run.append((a, b))
+                if Z == Y:
+                    a, b = -b % Z, a
+            if run:
+                runs.append(run)
+
+    def far(run):
+        a, b = run[0]
+        return -(min(a, Z - a) + min(b, Y - b))
+
+    return [(0, 0)] + [o for run in sorted(runs, key=far) for o in run]
+
+
 def iota(shape, axis):
     return lax.broadcasted_iota(jnp.int32, shape, axis)
 
 
-def kernel(dims, emb, lab, slab, cent, table, cos_out, sim_out,
-           send, recv, other, khi, klo, bias, frow, fpart, abuf, ans,
-           line_sem, plane_sem, own_sem,
+def kernel(dims, emb_hbm, lab_hbm, slab_hbm, cent_hbm, table, cos_out, sim_out,
+           emb, lab, slab, cent,
+           send, stage, out, recv, other, khi, klo, bias, frow, fpart, abuf, ans,
+           line_sem, load, gs, gr,
            fs, fr, ps, pr, ns, nr, xs_, xr, cs, cr, as_, ar, bs, br):
     Z, Y, X = dims
     nyz = Z * Y
@@ -50,6 +72,15 @@
     half_t = tiles // 2
     msg = 2 * tiles
     own = 2 * chips
+    offsets = yz_offsets(Z, Y)
+
+    loads = [
+        pltpu.make_async_copy(src, dst, load.at[i])
+        for i, (src, dst) in enumerate(
+            ((emb_hbm, emb), (lab_hbm, lab), (slab_hbm, slab), (cent_hbm, cent)))
+    ]
+    for copy in loads:
+        copy.start()
 
     dp = lax.axis_index("dp")
     x = lax.axis_index("cent")
@@ -75,6 +106,8 @@
         signal(barrier, z, y, (x + d) % X, core)
     signal(barrier, z, y, x, 1 - core)
 
+    loads[0].wait()
+    loads[1].wait()
     e = emb[...]
     unit = e * lax.rsqrt(jnp.sum(e * e, axis=1, keepdims=True) + epsilon)
 
@@ -86,7 +119,13 @@
     lcol = jnp.broadcast_to(lrow.astype(f32), (128, rows)).T[:, 0:1].astype(jnp.int32)
     earlier = (lcol == lrow) & (iota((rows, rows), 0) < iota((rows, rows), 1))
     rank = jnp.sum(jnp.where(earlier, 1.0, 0.0), axis=0, keepdims=True).astype(jnp.int32)
-    target = 2 * lrow + rank
+    lx, lyz = lrow // nyz, lrow % nyz
+    dx_row = (lx + X - x) % X
+    code = ((lyz // Y + Z - z) % Z) * Y + (lyz % Y + Y - y) % Y
+    q_row = jnp.zeros((1, rows), jnp.int32)
+    for q, (dz, dy) in enumerate(offsets):
+        q_row = jnp.where(code == dz * Y + dy, q, q_row)
+    target = 2 * (((q_row // GROUP) * X + dx_row) * GROUP + q_row % GROUP) + rank
     place = jnp.where(iota((own, rows), 0) == target, 1.0, 0.0)
     filled = jnp.sum(place, axis=1, keepdims=True) > 0.5
     slots = select_rows(place.astype(bf16), unit)
@@ -94,46 +133,56 @@
     for t in range(tiles):
         send[pl.ds(t, own, stride=tiles), :] = slots[:, t * 128:(t + 1) * 128]
 
+    block_rows = GROUP * msg
+    for g in range(n_group):
+        for dx in range(1, X):
+            pltpu.make_async_remote_copy(
+                src_ref=send.at[pl.ds((g * X + dx) * block_rows, block_rows)],
+                dst_ref=stage.at[pl.ds((g * (X - 1) + dx - 1) * block_rows, block_rows)],
+                send_sem=gs, recv_sem=gr.at[g],
+                device_id=device(z, y, (x + dx) % X, core), device_id_type=MESH,
+            ).start()
+
     pl.semaphore_wait(line_sem, Y - 1)
-    for d in range(1, X):
-        signal(plane_sem, z, y, (x + d) % X, core)
-    pl.semaphore_wait(plane_sem, X - 1)
-
-    def offset(q):
-        w = (q * 37) % nyz
-        return w // Y, w % Y
-
-    def forward(q, dx, g):
-        dz, dy = offset(q)
-        zz, yy, xx = (z + dz) % Z, (y + dy) % Y, (x + dx) % X
-        c = xx * nyz + zz * Y + yy
-        pltpu.make_async_remote_copy(
-            src_ref=send.at[pl.ds(c * msg, msg)],
-            dst_ref=recv.at[pl.ds((q * X + dx) * msg, msg)],
-            send_sem=fs, recv_sem=fr.at[g],
-            device_id=device(zz, yy, xx, core), device_id_type=MESH,
-        ).start()
-
-    own_copy = pltpu.make_async_copy(
-        send.at[pl.ds(me * msg, msg)], recv.at[pl.ds(0, msg)], own_sem)
-    own_copy.start()
-    for dx in range(1, X):
-        forward(0, dx, 0)
-
-    def forward_step(q, carry):
-        for dx in range(X):
-            forward(q, dx, q // GROUP)
-        return carry
-
-    lax.fori_loop(1, nyz, forward_step, 0)
-    own_copy.wait()
-
-    grows = GROUP * X * msg
-    krows = GROUP * X * 2
 
     def wait_rows(buf, start, count, sem):
         part = buf.at[pl.ds(start, count)]
         pltpu.make_async_copy(part, part, sem).wait()
+
+    zs = [(z + d) % Z for d in range(Z)]
+    ys = [(y + d) % Y for d in range(Y)]
+
+    def away(q):
+        dz, dy = offsets[q]
+        return device(zs[dz], ys[dy], x, core)
+
+    def back(q):
+        dz, dy = offsets[q]
+        return device(zs[-dz % Z], ys[-dy % Y], x, core)
+
+    for g in range(n_group):
+        wait_rows(stage, g * (X - 1) * block_rows, (X - 1) * block_rows, gr.at[g])
+        for j in range(GROUP):
+            q = g * GROUP + j
+            into = recv if q == 0 else out
+            for dx in range(X):
+                if dx == 0:
+                    piece = send[pl.ds(g * X * block_rows + j * msg, msg), :]
+                else:
+                    piece = stage[pl.ds((g * (X - 1) + dx - 1) * block_rows + j * msg, msg), :]
+                into[pl.ds((q * X + dx) * msg, msg), :] = piece
+        for j in range(GROUP):
+            q = g * GROUP + j
+            if q > 0:
+                pltpu.make_async_remote_copy(
+                    src_ref=out.at[pl.ds(q * X * msg, X * msg)],
+                    dst_ref=recv.at[pl.ds(q * X * msg, X * msg)],
+                    send_sem=fs, recv_sem=fr.at[g],
+                    device_id=away(q), device_id_type=MESH,
+                ).start()
+
+    grows = GROUP * X * msg
+    krows = GROUP * X * 2
 
     def take(buf, g, base, total):
         columns = []
@@ -159,7 +208,7 @@
     mine = jnp.zeros((1, width), f32)
     theirs = jnp.zeros((1, width), f32)
     for g in range(n_group):
-        missing = msg if g == 0 else 0
+        missing = X * msg if g == 0 else 0
         wait_rows(recv, g * grows + missing, grows - missing, fr.at[g])
         pltpu.make_async_remote_copy(
             src_ref=recv.at[pl.ds(g * grows, grows)],
@@ -181,16 +230,12 @@
         b = fresh[:, (half_t + t) * 128:(half_t + t + 1) * 128]
         frow[pl.ds(me * half_t + t, 1), :] = jnp.where(core == 0, a, b)
 
-    def fresh_step(q, carry):
-        dz, dy = offset(q)
+    for q in range(1, nyz):
         part = frow.at[pl.ds(me * half_t, half_t)]
         pltpu.make_async_remote_copy(
             src_ref=part, dst_ref=part, send_sem=ns, recv_sem=nr,
-            device_id=device((z + dz) % Z, (y + dy) % Y, x, core), device_id_type=MESH,
-        ).start()
-        return carry
-
-    lax.fori_loop(1, nyz, fresh_step, 0)
+            device_id=away(q), device_id_type=MESH,
+        ).start()
 
     qh = khi[0:own, :]
     ql = klo[0:own, :]
@@ -244,16 +289,12 @@
     abuf[...] = jnp.sum(spread, axis=1).reshape(nyz, 128)
     ans[pl.ds(me, 1), :] = abuf[0:1, :]
 
-    def answer_step(q, carry):
-        dz, dy = offset(q)
+    for q in range(1, nyz):
         pltpu.make_async_remote_copy(
             src_ref=abuf.at[pl.ds(q, 1)], dst_ref=ans.at[pl.ds(me, 1)],
             send_sem=as_, recv_sem=ar,
-            device_id=device((z + Z - dz) % Z, (y + Y - dy) % Y, x, core), device_id_type=MESH,
-        ).start()
-        return carry
-
-    lax.fori_loop(1, nyz, answer_step, 0)
+            device_id=back(q), device_id_type=MESH,
+        ).start()
 
     for dx in range(1, X):
         wait_rows(frow, ((x + X - dx) % X) * xrows, xrows, xr.at[dx])
@@ -267,6 +308,8 @@
             device_id=device(z, y, (x + dx) % X, core), device_id_type=MESH,
         ).start()
 
+    loads[2].wait()
+    loads[3].wait()
     for dx in range(X):
         wait_rows(fpart, ((x + X - dx) % X) * xrows, xrows, cr.at[dx])
     low, high = [], []
@@ -299,13 +342,25 @@
     sim_out[...] = pick(0)
     cos_out[...] = pick(1)
 
-    wait_rows(send, 0, (chips - 1) * msg, fs)
+    wait_rows(send, 0, n_group * (X - 1) * block_rows, gs)
+    wait_rows(out, 0, (nyz - 1) * X * msg, fs)
     wait_rows(recv, 0, n_group * grows, ps)
     wait_rows(frow, 0, (nyz - 1) * half_t, ns)
     wait_rows(frow, 0, (X - 1) * xrows, xs_)
     wait_rows(frow, 0, X * xrows, cs)
     wait_rows(ans, 0, nyz - 1, as_)
     wait_rows(ans, 0, (X - 1) * nyz, bs)
+
+
+def store(table, cos, sim, table_out, cos_out, sim_out, sems):
+    copies = [
+        pltpu.make_async_copy(src, dst, sems.at[i])
+        for i, (src, dst) in enumerate(((table, table_out), (cos, cos_out), (sim, sim_out)))
+    ]
+    for copy in copies:
+        copy.start()
+    for copy in copies:
+        copy.wait()
 
 
 def local(dims, embeddings, assignment, slab_ids, centroids):
@@ -318,16 +373,24 @@
     linear = 2 * chips * tiles
     dma = pltpu.SemaphoreType.DMA
     vmem = pl.BlockSpec(memory_space=pltpu.VMEM)
-    table, cos, sim = pl.pallas_call(
+    hbm = pl.BlockSpec(memory_space=pl.ANY)
+    outs = (
+        jax.ShapeDtypeStruct(centroids.shape, f32),
+        jax.ShapeDtypeStruct((1, rows), f32),
+        jax.ShapeDtypeStruct((1, rows), f32),
+    )
+    results = pl.pallas_call(
         functools.partial(kernel, dims),
-        out_shape=(
-            jax.ShapeDtypeStruct(centroids.shape, f32),
-            jax.ShapeDtypeStruct((1, rows), f32),
-            jax.ShapeDtypeStruct((1, rows), f32),
-        ),
-        in_specs=[vmem] * 4,
+        out_shape=outs,
+        in_specs=[pl.BlockSpec(memory_space=pltpu.HBM)] * 4,
         out_specs=(vmem,) * 3,
         scratch_shapes=[
+            pltpu.VMEM((rows, width), f32),
+            pltpu.VMEM((1, rows), jnp.int32),
+            pltpu.VMEM((1, chips), jnp.int32),
+            pltpu.VMEM(centroids.shape, f32),
+            pltpu.VMEM((linear, 128), f32),
+            pltpu.VMEM((linear // X * (X - 1), 128), f32),
             pltpu.VMEM((linear, 128), f32),
             pltpu.VMEM((linear, 128), f32),
             pltpu.VMEM((linear, 128), f32),
@@ -339,16 +402,22 @@
             pltpu.VMEM((nyz, 128), f32),
             pltpu.VMEM((chips, 128), f32),
             pltpu.SemaphoreType.REGULAR,
-            pltpu.SemaphoreType.REGULAR,
-            dma,
+            dma((4,)), dma, dma((n_group,)),
             dma, dma((n_group,)), dma, dma((n_group,)),
             dma, dma, dma, dma((X,)), dma, dma((X,)),
             dma, dma, dma, dma((X,)),
         ],
         compiler_params=pltpu.CompilerParams(
-            collective_id=0, has_side_effects=True, vmem_limit_bytes=40 * 2**20
+            collective_id=0, has_side_effects=True, vmem_limit_bytes=107 * 2**19
         ),
     )(embeddings, assignment.reshape(1, rows), slab_ids.reshape(1, chips), centroids)
+    table, cos, sim = pl.pallas_call(
+        store,
+        out_shape=outs,
+        in_specs=[vmem] * 3,
+        out_specs=(hbm,) * 3,
+        scratch_shapes=[dma((3,))],
+    )(*results)
     return table, cos.reshape(rows), sim.reshape(rows)
 
 

time: 86.9 us -> 88.4 us (1.017)
  Pallas kernels: 81.3 us -> 84.6 us
  local copies, waits for them, and re-layouts: 4.68 us -> 2.02 us
    pallas_call x1 -> x2, Pallas kernels: 81.3 us -> 84.6 us  [the longest x1 82.8 us: local(): pl.pallas_call(functools.partial(kernel, dims), out_shape=outs, in_specs=...]
    unnamed x11 -> x10, local copies, waits for them, and re-layouts: 4.68 us -> 2.02 us
where the time goes in v2:
time: 88.4 us; the launch traced here: 87.3 us
  Pallas kernels  84.6 us (96%)
  local copies, waits for them, and re-layouts  2.02 us (2%)
    pallas_call x1, Pallas kernels, local(): pl.pallas_call(functools.partial(kernel, dims), out_shape=outs, in_specs=...  82.8 us
    unnamed x10, local copies, waits for them, and re-layouts  2.02 us
    pallas_call x1, Pallas kernels, local(): pl.pallas_call(store, out_shape=outs, in_specs=[vmem] * 3, out_specs=(hbm...  1.77 us

profile of v2, /device:TPU:1, one launch (start us, length us, event | category | flops | bytes accessed | tf_op | source)
XLA Modules:
  0.0 87.3 jit_solution(11820828981101635842)
XLA Ops:
  0.6 0.0 copy-start.2
  0.6 0.0 copy-start.1
  0.7 0.7 copy-done.2
  1.3 0.0 copy-done.1
  1.3 82.8 %shard_map.67 = (f32[128,768]{1,0:T(8,128)S(1)}, f32[1,256]{1,0:T(1,128)S(1)}, f32[1,256]{1,0:T(1,128)S(1)}) custom-call(f32[256,768]{1,0:T(8,128)} %emb_hbm.1, s32[1,256]{1,0:T(1,128)S(1)} %bitcast.4, s32[1,256]{1,0:T(1,128)S(1)} %bitcast.5, f32[128,768]{1,0:T(8,128)} %cent_hbm.1), custom_call_target="tpu_custom_call" | custom-call | tf_op jit(solution)/shard_map/pallas_call | solution.py:382
  84.2 0.0 copy-start
  84.2 0.7 copy-done
  84.9 0.0 copy-start.3
  84.9 0.0 copy-start.4
  84.9 0.5 copy-done.3
  85.5 0.1 copy-done.4
  85.5 1.8 %shard_map.68 = (f32[128,768]{1,0:T(8,128)}, f32[1,256]{1,0:T(1,128)}, f32[1,256]{1,0:T(1,128)}) custom-call(f32[128,768]{1,0:T(8,128)} %copy-done, f32[1,256]{1,0:T(1,128)} %copy-done.3, f32[1,256]{1,0:T(1,128)} %copy-done.4), custom_call_target="tpu_custom_call" | custom-call | tf_op jit(solution)/shard_map/pallas_call | solution.py:414
Async XLA Ops:
  0.6 0.7 copy-start.2
  0.6 0.7 copy-start.1
  84.2 0.8 copy-start
  84.9 0.5 copy-start.3
  84.9 0.6 copy-start.4

commit v3 on v0

v3 whole, which is shorter than its diff:
```python
import functools

import jax
import jax.numpy as jnp
from jax import lax
from jax.experimental import pallas as pl
from jax.experimental.pallas import tpu as pltpu
from jax.sharding import PartitionSpec as P

epsilon = 1e-06
Z, Y, X = 8, 8, 4
GROUP = 8
KERNEL_BYTES = 105 * 2**19
SENTINEL = 4.0
MESH = pl.DeviceIdType.MESH
f32, bf16 = jnp.float32, jnp.bfloat16


def split3(v):
    hi = v.astype(bf16)
    rest = v - hi.astype(f32)
    mid = rest.astype(bf16)
    lo = (rest - mid.astype(f32)).astype(bf16)
    return hi, mid, lo


def select_rows(onehot, v):
    hi, mid, lo = split3(v)
    dot = functools.partial(jnp.dot, preferred_element_type=f32)
    return dot(onehot, hi) + dot(onehot, mid) + dot(onehot, lo)


def plan(Z, Y):
    def step(d, other, n):
        return 0 if 2 * d != n else (1 if other % 2 == 0 else -1)

    ties = {}
    for dz in range(Z):
        for dy in range(Y):
            shift = (step(dz, dy, Z), step(dy, dz, Y))
            if shift != (0, 0):
                ties.setdefault(shift, []).append((dz, dy))
    offsets, batches = [(0, 0)], []
    for shift in ((1, 1), (1, 0), (0, 1), (-1, 0), (0, -1)):
        batches.append((len(offsets), len(ties[shift])) + shift)
        offsets += ties[shift]
    seen, runs = set(offsets), []
    for dz in range(Z):
        for dy in range(Y):
            run, a, b = [], dz, dy
            for _ in range(4):
                if (a, b) not in seen:
                    seen.add((a, b))
                    run.append((a, b))
                a, b = -b % Z, a
            if run:
                runs.append(run)
    runs.sort(key=lambda run: -sum(min(d, Z - d) for d in run[0]))
    rest = [o for run in runs for o in run]
    return offsets + rest, batches


def iota(shape, axis):
    return lax.broadcasted_iota(jnp.int32, shape, axis)


def position():
    dp = lax.axis_index("dp")
    return dp, lax.axis_index("cent"), dp % 2


def wait_rows(buf, start, count, sem):
    part = buf.at[pl.ds(start, count)]
    pltpu.make_async_copy(part, part, sem).wait()


def ranks(lrow):
    rows = lrow.shape[1]
    lcol = jnp.broadcast_to(lrow.astype(f32), (128, rows)).T[:, 0:1].astype(jnp.int32)
    earlier = (lcol == lrow) & (iota((rows, rows), 0) < iota((rows, rows), 1))
    return jnp.sum(jnp.where(earlier, 1.0, 0.0), axis=0, keepdims=True).astype(jnp.int32)


def exchange(dims, emb_hbm, lab_hbm, frow, fpart, ans,
             emb, lab, send, stage, out, recv, other, khi, klo, qht, qlt, bias,
             abuf, ay, ab, az,
             line_sem, plane_sem, load, gs, gr, fs, fr, ps, pr,
             nys, nyr, nzs, nzr, nxs, nxr, ncs, ncr, ays, ayr, azs, azr, axs, axr):
    Z, Y, X = dims
    nyz = Z * Y
    chips = nyz * X
    n_group = nyz // GROUP
    rows, width = emb.shape
    tiles = width // 128
    half_t = tiles // 2
    msg = 2 * tiles
    own = 2 * chips
    offsets, batches = plan(Z, Y)
    tied = sum(n for _, n, _, _ in batches) + 1

    loads = [pltpu.make_async_copy(lab_hbm, lab, load.at[0])]
    part = rows // 4
    loads += [
        pltpu.make_async_copy(
            emb_hbm.at[pl.ds(i * part, part)], emb.at[pl.ds(i * part, part)], load.at[1 + i])
        for i in range(4)
    ]
    for copy in loads:
        copy.start()

    dp, x, core = position()
    yz = dp // 2
    y = yz % Y
    z = yz // Y
    me = x * nyz + yz
    zs = [(z + d) % Z for d in range(Z)]
    ys = [(y + d) % Y for d in range(Y)]
    partner = (yz * 2 + 1 - core, x)

    def at(dz, dy, dx=0):
        return ((zs[dz % Z] * Y + ys[dy % Y]) * 2 + core, (x + dx) % X)

    def signal(sem, where):
        pl.semaphore_signal(sem, inc=1, device_id=where, device_id_type=MESH)

    def start(src, dst, send_sem, recv_sem, where):
        pltpu.make_async_remote_copy(
            src_ref=src, dst_ref=dst, send_sem=send_sem, recv_sem=recv_sem,
            device_id=where, device_id_type=MESH,
        ).start()

    barrier = pltpu.get_barrier_semaphore()
    for d in range(1, Z):
        signal(barrier, at(d, 0))
    for d in range(1, Y):
        signal(barrier, at(0, d))
    for d in range(1, X):
        signal(barrier, at(0, 0, d))
    signal(barrier, partner)

    loads[0].wait()
    lrow = lab[...]
    rank = ranks(lrow)
    lx, lyz = lrow // nyz, lrow % nyz
    dx_row = (lx + X - x) % X
    code = ((lyz // Y + Z - z) % Z) * Y + (lyz % Y + Y - y) % Y
    first_slot = jnp.zeros((1, rows), jnp.int32)
    per_dx = jnp.ones((1, rows), jnp.int32)
    for q, (dz, dy) in enumerate(offsets):
        if q == 0 or q >= tied:
            first_slot = jnp.where(code == dz * Y + dy, q * X, first_slot)
    for q0, n, _, _ in batches:
        for q in range(q0, q0 + n):
            here = code == offsets[q][0] * Y + offsets[q][1]
            first_slot = jnp.where(here, q0 * X + q - q0, first_slot)
            per_dx = jnp.where(here, n, per_dx)
    target = 2 * (first_slot + dx_row * per_dx) + rank

    pl.semaphore_wait(barrier, Z + Y + X - 2)
    for d in range(1, Y):
        signal(line_sem, at(0, d))

    for copy in loads[1:]:
        copy.wait()
    e = emb[...]
    unit = e * lax.rsqrt(jnp.sum(e * e, axis=1, keepdims=True) + epsilon)
    parts = split3(unit)

    n_chunk = min(4, n_group)
    chunk = own // n_chunk
    chunk_q = nyz // n_chunk

    def fill(i):
        low = i * chunk
        place = jnp.where(iota((chunk, rows), 0) + low == target, 1.0, 0.0)
        filled = jnp.sum(place, axis=1, keepdims=True) > 0.5
        place = place.astype(bf16)
        slots = sum(jnp.dot(place, p, preferred_element_type=f32) for p in parts)
        slots = jnp.where(filled, slots, SENTINEL)
        for t in range(tiles):
            send[pl.ds(low * tiles + t, chunk, stride=tiles), :] = (
                slots[:, t * 128:(t + 1) * 128])

    def straight(q, dx):
        piece = pl.ds((q * X + dx) * msg, msg)
        start(send.at[piece], recv.at[piece], fs, fr.at[q // GROUP], at(*offsets[q], dx))

    def straight_all(i):
        def step(dx, carry):
            for q in range(i * chunk_q, (i + 1) * chunk_q):
                straight(q, dx)
            return carry
        lax.fori_loop(1, X, step, 0)

    fill(1)
    pl.semaphore_wait(line_sem, Y - 1)
    for d in range(1, X):
        signal(plane_sem, at(0, 0, d))
    for q in range(chunk_q, 2 * chunk_q):
        straight(q, 0)
    fill(0)
    pl.semaphore_wait(plane_sem, X - 1)
    for b, (q0, n, sz, sy) in enumerate(batches):
        for dx in range(X):
            piece = pl.ds((q0 * X + dx * n) * msg, n * msg)
            start(send.at[piece], stage.at[piece], gs, gr.at[b], at(sz, sy, dx))
    for dx in range(1, X):
        straight(0, dx)
    recv[0:msg, :] = send[0:msg, :]
    straight_all(1)
    for b, (q0, n, sz, sy) in enumerate(batches):
        wait_rows(stage, q0 * X * msg, X * n * msg, gr.at[b])
        for q in range(q0, q0 + n):
            for dx in range(X):
                piece = stage[pl.ds((q0 * X + dx * n + q - q0) * msg, msg), :]
                out[pl.ds((q * X + dx) * msg, msg), :] = piece
        for q in range(q0, q0 + n):
            piece = pl.ds(q * X * msg, X * msg)
            start(out.at[piece], recv.at[piece], fs, fr.at[q // GROUP],
                  at(offsets[q][0] - sz, offsets[q][1] - sy))
    for i in range(2, n_chunk):
        fill(i)
        for q in range(i * chunk_q, (i + 1) * chunk_q):
            straight(q, 0)
        straight_all(i)

    grows = GROUP * X * msg
    krows = GROUP * X * 2

    def take(buf, g, base, total):
        columns = []
        dead = None
        for t in range(tiles):
            pieces = []
            for dx in range(X):
                for s in range(2):
                    first = g * grows + dx * msg + s * tiles + t
                    pieces.append(buf[pl.ds(first, GROUP, stride=X * msg), :])
            v = jnp.concatenate(pieces, axis=0)
            if dead is None:
                dead = v > 2.0
                bias[pl.ds(base + g * krows, krows), :] = jnp.where(dead, -4.0, 0.0)
            v = jnp.where(dead, 0.0, v)
            hi = v.astype(bf16)
            lo = (v - hi.astype(f32)).astype(bf16)
            khi[pl.ds(base + g * krows, krows), t * 128:(t + 1) * 128] = hi
            klo[pl.ds(base + g * krows, krows), t * 128:(t + 1) * 128] = lo
            columns.append(jnp.sum(v, axis=0, keepdims=True))
        return total + jnp.concatenate(columns, axis=1)

    mine = jnp.zeros((1, width), f32)
    theirs = jnp.zeros((1, width), f32)
    per_chunk = n_group // n_chunk
    order = [g for i in [1, 0] + list(range(2, n_chunk))
             for g in range(i * per_chunk, (i + 1) * per_chunk)]
    done = set()
    for g in order:
        missing = msg if g == 0 else 0
        wait_rows(recv, g * grows + missing, grows - missing, fr.at[g])
        piece = pl.ds(g * grows, grows)
        start(recv.at[piece], other.at[piece], ps, pr.at[g], partner)
        mine = take(recv, g, 0, mine)
        done.add(g)
        block = g * krows // 128
        members = [h for h in range(n_group) if h * krows // 128 == block]
        if done.issuperset(members):
            top = pl.ds(block * 128, min(128, own))
            for t in range(tiles):
                lanes = pl.ds(t * 128, 128)
                qht[lanes, top] = khi[top, lanes].astype(f32).T.astype(bf16)
                qlt[lanes, top] = klo[top, lanes].astype(f32).T.astype(bf16)
        wait_rows(other, g * grows, grows, pr.at[g])
        theirs = take(other, g, own, theirs)

    sums = mine + theirs
    fresh = sums * lax.rsqrt(jnp.sum(sums * sums, axis=1, keepdims=True) + epsilon)
    for t in range(half_t):
        a = fresh[:, t * 128:(t + 1) * 128]
        b = fresh[:, (half_t + t) * 128:(half_t + t + 1) * 128]
        frow[pl.ds(me * half_t + t, 1), :] = jnp.where(core == 0, a, b)
    piece = pl.ds(me * half_t, half_t)
    for d in range(1, Y):
        start(frow.at[piece], frow.at[piece], nys, nyr, at(0, d))
    fh = fresh.astype(bf16)
    khi[2 * own:2 * own + 16, :] = jnp.broadcast_to(fresh, (16, width)).astype(bf16)
    klo[2 * own:2 * own + 16, :] = jnp.broadcast_to(
        fresh - fh.astype(f32), (16, width)).astype(bf16)

    def product(first, count):
        kh = khi[first:first + count, :]
        kl = klo[first:first + count, :]
        dot = functools.partial(jnp.dot, preferred_element_type=f32)
        return dot(kh, qht[...]) + dot(kh, qlt[...]) + dot(kl, qht[...])

    def closest(s, first):
        off = bias[first:first + own, :]
        s = s + (jnp.concatenate([off] * (own // 128), axis=1) if own > 128 else off[:, :own])
        if first == 0:
            s = jnp.where(iota((own, own), 0) == iota((own, own), 1), -4.0, s)
        return jnp.max(s, axis=0, keepdims=True)

    best = jnp.maximum(closest(product(0, own), 0), -1.0)

    yrows = Y * half_t
    wait_rows(frow, 0, (Y - 1) * half_t, nyr)
    piece = pl.ds((x * nyz + z * Y) * half_t, yrows)
    for d in range(1, Z):
        start(frow.at[piece], frow.at[piece], nzs, nzr, at(d, 0))

    s = product(own, own + 16)
    best = jnp.maximum(best, closest(s[:own, :], own))
    cos = s[own:own + 1, :]

    xs = (iota((128, own), 1) // GROUP) % (2 * X)
    lane_of = (xs // 2) * 8 + (xs % 2) * 2
    j = iota((128, own), 0)
    spread = jnp.where(j == lane_of, best, jnp.where(j == lane_of + 1, cos, 0.0))
    spread = spread.T.reshape(n_group, 2 * X, GROUP, 128)
    spread = jnp.sum(spread, axis=1).reshape(nyz, 128)
    for q, (dz, dy) in enumerate(offsets):
        abuf[dy * Z + dz:dy * Z + dz + 1, :] = spread[q:q + 1, :]
    for d in range(1, Y):
        start(abuf.at[pl.ds(d * Z, Z)], ay.at[pl.ds(y * Z, Z)], ays, ayr, at(0, -d))
    ay[pl.ds(y * Z, Z), :] = abuf[0:Z, :]

    xrows = nyz * half_t
    hrows = xrows // 2

    def block_of(dx, half):
        return pl.ds(((x + dx) % X) * xrows + half * hrows, hrows)

    def along(dx, half, sem, to):
        piece = block_of(dx, half)
        start(frow.at[piece], frow.at[piece], nxs, nxr.at[sem], at(0, 0, to))

    def pass_on(dx):
        piece = pl.ds(((x + dx) % X) * xrows, xrows)
        start(frow.at[piece], fpart.at[piece], ncs, ncr.at[dx], partner)

    def landed(dx, half, sem):
        wait_rows(frow, ((x + dx) % X) * xrows + half * hrows, hrows, nxr.at[sem])

    wait_rows(frow, 0, (Z - 1) * yrows, nzr)
    along(0, 0, 0, 1)
    if X > 2:
        along(0, 1, 2, X - 1)
    along(0, 1, 1, 1)
    if X > 2:
        along(0, 0, 3, X - 1)
    pass_on(0)
    if X > 2:
        landed(X - 1, 0, 0)
        along(X - 1, 0, 4, 1)
        landed(1, 1, 2)
        along(1, 1, 5, X - 1)

    wait_rows(ay, 0, (Y - 1) * Z, ayr)
    for dz in range(Z):
        ab[dz * Y:(dz + 1) * Y, :] = ay[pl.ds(dz, Y, stride=Z), :]
    for d in range(1, Z):
        start(ab.at[pl.ds(d * Y, Y)], az.at[pl.ds(z * Y, Y)], azs, azr, at(-d, 0))
    az[pl.ds(z * Y, Y), :] = ab[0:Y, :]

    if X > 2:
        landed(X - 1, 1, 1)
        pass_on(X - 1)
        landed(1, 0, 3)
        pass_on(1)
    else:
        landed(1, 0, 0)
        landed(1, 1, 1)
        pass_on(1)

    wait_rows(az, 0, (Z - 1) * Y, azr)
    wait_rows(ay, 0, (Y - 1) * Z, ays)
    turned = jnp.concatenate([az[...], jnp.zeros((128 - nyz, 128), f32)], axis=0).T
    abuf[0:8 * X, :] = turned[0:8 * X, :]
    for d in range(1, X):
        start(abuf.at[pl.ds(d * 8, 8)], ans.at[pl.ds(x * 8, 8)], axs, axr, at(0, 0, X - d))
    ans[pl.ds(x * 8, 8), :] = abuf[0:8, :]

    if X > 2:
        landed(2, 0, 4)
        landed(2, 1, 5)
        pass_on(2)
    for dx in range(X):
        wait_rows(fpart, ((x + dx) % X) * xrows, xrows, ncr.at[dx])
    wait_rows(ans, 0, (X - 1) * 8, axr)

    wait_rows(send, 0, (tied - 1) * X * msg, gs)
    wait_rows(send, 0, (chips - 1) * msg, fs)
    wait_rows(recv, 0, n_group * grows, ps)
    wait_rows(frow, 0, (Y - 1) * half_t, nys)
    wait_rows(frow, 0, (Z - 1) * yrows, nzs)
    wait_rows(frow, 0, (X - 1) * xrows, nxs)
    wait_rows(frow, 0, X * xrows, ncs)
    wait_rows(az, 0, (Z - 1) * Y, azs)
    wait_rows(ans, 0, (X - 1) * 8, axs)


def finish(dims, frow, fpart, ans, lab, slab, cent, table_hbm, cos_hbm, sim_hbm,
           table, cos_out, sim_out, put):
    Z, Y, X = dims
    nyz = Z * Y
    chips = nyz * X
    trows, width = cent.shape
    half_t = width // 256
    dp, x, core = position()
    rows = lab.shape[1]

    low, high = [], []
    for t in range(half_t):
        a = frow[pl.ds(t, chips, stride=half_t), :]
        b = fpart[pl.ds(t, chips, stride=half_t), :]
        low.append(jnp.where(core == 0, a, b))
        high.append(jnp.where(core == 0, b, a))
    full = jnp.concatenate(low + high, axis=1)
    row_id = (dp * X + x) * trows + iota((trows, chips), 0)
    hit = jnp.where(row_id == slab[...], 1.0, 0.0)
    named = jnp.sum(hit, axis=1, keepdims=True) > 0.5
    table[...] = jnp.where(named, select_rows(hit.astype(bf16), full), cent[...])
    pairs = [(cos_out, cos_hbm), (sim_out, sim_hbm)]
    part = trows // 4
    pairs += [
        (table.at[pl.ds(i * part, part)], table_hbm.at[pl.ds(i * part, part)]) for i in range(4)]
    puts = [pltpu.make_async_copy(src, dst, put.at[i]) for i, (src, dst) in enumerate(pairs)]
    for copy in puts[2:]:
        copy.start()

    lrow = lab[...]
    rank = ranks(lrow)
    spot = (lrow // nyz) * 128 + lrow % nyz
    member = jnp.where(iota((X * 128, rows), 0) == spot, 1.0, 0.0).astype(bf16)
    got = jnp.concatenate([ans[i * 8:(i + 1) * 8, :] for i in range(X)], axis=1)
    got = jnp.concatenate([got, jnp.zeros_like(got)], axis=0)
    got = sum(jnp.dot(p, member, preferred_element_type=f32) for p in split3(got))
    sim_out[...] = jnp.where(rank == 0, got[0:1, :], got[2:3, :])
    cos_out[...] = jnp.where(rank == 0, got[1:2, :], got[3:4, :])
    puts[0].start()
    puts[1].start()
    for copy in puts:
        copy.wait()


def local(dims, embeddings, assignment, slab_ids, centroids):
    Z, Y, X = dims
    nyz = Z * Y
    chips = nyz * X
    rows, width = embeddings.shape
    tiles = width // 128
    n_group = nyz // GROUP
    n_batch = len(plan(Z, Y)[1])
    linear = 2 * chips * tiles
    half = chips * tiles // 2
    dma = pltpu.SemaphoreType.DMA
    vmem = pl.BlockSpec(memory_space=pltpu.VMEM)
    hbm = pl.BlockSpec(memory_space=pl.ANY)
    shape = jax.ShapeDtypeStruct
    regular = pltpu.SemaphoreType.REGULAR
    labels = assignment.reshape(1, rows)

    given = pl.pallas_call(
        functools.partial(exchange, dims),
        out_shape=(
            shape((half, 128), f32),
            shape((half, 128), f32),
            shape((8 * X, 128), f32),
        ),
        in_specs=[hbm] * 2,
        out_specs=(vmem,) * 3,
        scratch_shapes=[
            pltpu.VMEM((rows, width), f32),
            pltpu.VMEM((1, rows), jnp.int32),
            pltpu.VMEM((linear, 128), f32),
            pltpu.VMEM((linear, 128), f32),
            pltpu.VMEM((linear, 128), f32),
            pltpu.VMEM((linear, 128), f32),
            pltpu.VMEM((linear, 128), f32),
            pltpu.VMEM((4 * chips + 16, width), bf16),
            pltpu.VMEM((4 * chips + 16, width), bf16),
            pltpu.VMEM((width, 2 * chips), bf16),
            pltpu.VMEM((width, 2 * chips), bf16),
            pltpu.VMEM((4 * chips, 128), f32),
            pltpu.VMEM((max(nyz, 8 * X), 128), f32),
            pltpu.VMEM((nyz, 128), f32),
            pltpu.VMEM((nyz, 128), f32),
            pltpu.VMEM((nyz, 128), f32),
            regular, regular,
            dma((5,)), dma, dma((n_batch,)),
            dma, dma((n_group,)), dma, dma((n_group,)),
            dma, dma, dma, dma, dma, dma((6,)), dma, dma((X,)),
            dma, dma, dma, dma, dma, dma,
        ],
        compiler_params=pltpu.CompilerParams(
            collective_id=0, has_side_effects=True, vmem_limit_bytes=KERNEL_BYTES),
    )(embeddings, labels)

    table, cos, sim = pl.pallas_call(
        functools.partial(finish, dims),
        out_shape=(
            shape(centroids.shape, f32),
            shape((1, rows), f32),
            shape((1, rows), f32),
        ),
        in_specs=[vmem] * 6,
        out_specs=(hbm,) * 3,
        scratch_shapes=[
            pltpu.VMEM(centroids.shape, f32),
            pltpu.VMEM((1, rows), f32),
            pltpu.VMEM((1, rows), f32),
            dma((6,)),
        ],
        compiler_params=pltpu.CompilerParams(vmem_limit_bytes=32 * 2**20),
    )(*given, labels, slab_ids.reshape(1, chips), centroids)
    return table, cos.reshape(rows), sim.reshape(rows)


def solution(mesh, dims=(Z, Y, X)):
    placed = (P(("dp", "cent"), None), P(("dp", "cent"), None), P(), P(("dp", "cent"), None))
    return jax.shard_map(
        functools.partial(local, dims),
        mesh=mesh,
        in_specs=placed,
        out_specs=(P(("dp", "cent"), None), P(("dp", "cent")), P(("dp", "cent"))),
        check_vma=False,
    )
```

time: 396 us -> 90.6 us (0.23)
  waiting for transfers between devices: 297 us -> 0 us
  Pallas kernels: 0 us -> 87.1 us
  starting transfers between devices: 35.2 us -> 0 us
  local copies, waits for them, and re-layouts: 17.1 us -> 1.34 us
  between operations: 15.7 us -> 0.66 us
  matrix products: 11.8 us -> 0 us
  blocking collectives: 9.66 us -> 0 us
  other arithmetic: 8.48 us -> 0 us
    psum x1 -> x0, waiting for transfers between devices: 233 us -> none  [local(): totals = lax.psum(partial_value, ('dp', 'cent'))]
    pallas_call x0 -> x2, Pallas kernels: none -> 87.1 us  [the longest x1 85.8 us: local(): pl.pallas_call(functools.partial(exchange, dims), out_shape=(shape((half,...]
    all_to_all x3 -> x0, waiting for transfers between devices: 64.4 us -> none  [the longest x1 39.9 us: local(): lax.all_to_all(outgoing, 'dp', split_axis=1, concat_axis=1, tiled=True)]
    all_to_all x3 -> x0, starting transfers between devices: 35.1 us -> none  [the longest x1 18.4 us: local(): lax.all_to_all(outgoing, 'dp', split_axis=1, concat_axis=1, tiled=True)]
    dot_general x3 -> x0, matrix products: 11.8 us -> none  [the longest x1 7.82 us: cluster_sims(): jnp.einsum('cqe,cke->cqk', queries, keys, precision=lax.Precision.HIGHEST...]
    all_gather x1 -> x0, blocking collectives: 9.66 us -> none  [local(): key_live = lax.all_gather(query_live, 'cent', axis=1, tiled=True)]
    reshape x7 -> x0, local copies, waits for them, and re-layouts: 8.22 us -> none  [the longest x2 3.92 us: local(): outgoing = outgoing.reshape(cl_own, n_dp, cap, width)]
    gather x2 -> x0, local copies, waits for them, and re-layouts: 3.97 us -> none  [the longest x1 2.02 us: local(): centroid_cos = jnp.sum(unit * jnp.take(fresh, labels, axis=0), axis=1)]
  transfers between devices with their start and end apart: 5 -> 0, of which waited for: 4 -> 0; matrix products, arithmetic and copies ran while one was open for 4% -> 0% of each run, Pallas kernels for 0% -> 0%
where the time goes in v3:
time: 90.6 us; the launch traced here: 89.1 us
  Pallas kernels  87.1 us (96%)
  local copies, waits for them, and re-layouts  1.34 us (1%)
    pallas_call x1, Pallas kernels, local(): pl.pallas_call(functools.partial(exchange, dims), out_shape=(shape((half,...  85.8 us

profile of v3, /device:TPU:1, one launch (start us, length us, event | category | flops | bytes accessed | tf_op | source)
XLA Modules:
  0.0 89.1 jit_solution(17050535335082943391)
XLA Ops:
  0.6 0.0 copy-start.1
  0.6 0.7 copy-done.1
  1.3 0.0 copy-start
  1.3 85.8 %shard_map.67 = (f32[768,128]{1,0:T(8,128)S(1)}, f32[768,128]{1,0:T(8,128)S(1)}, f32[32,128]{1,0:T(8,128)S(1)}) custom-call(f32[256,768]{1,0:T(8,128)} %emb_hbm.1, s32[1,256]{1,0:T(1,128)S(1)} %bitcast.4), custom_call_target="tpu_custom_call" | custom-call | tf_op jit(solution)/shard_map/pallas_call | solution.py:462
  87.1 0.0 copy-start.2
  87.1 0.0 copy-done
  87.1 0.7 copy-done.2
  87.8 1.3 %shard_map.68 = (f32[128,768]{1,0:T(8,128)}, f32[1,256]{1,0:T(1,128)}, f32[1,256]{1,0:T(1,128)}) custom-call(f32[768,128]{1,0:T(8,128)S(1)} %get-tuple-element.9.frow, f32[768,128]{1,0:T(8,128)S(1)} %get-tuple-element.10.fpart, f32[32,128]{1,0:T(8,128)S(1)} %get-tuple-element.11.ans, s32[1,256]{1,0:T(1,128)S(1)} %bitcast.5, s32[1,256]{1,0:T(1,128)S(1)} %bitcast.6, ...), custom_call_target="tpu_custom_call" | custom-call | tf_op jit(solution)/shard_map/pallas_call | solution.py:498
Async XLA Ops:
  0.6 0.7 copy-start.1
  1.3 85.8 %copy-start = (f32[128,768]{1,0:T(8,128)S(1)}, f32[128,768]{1,0:T(8,128)}, u32[]{:S(2)}) copy-start(f32[128,768]{1,0:T(8,128)} %cent.1) | copy-start | bytes 1179652
  87.1 0.7 copy-start.2

commit v4 on v3

--- a/solution.py
+++ b/solution.py
@@ -12,6 +12,7 @@
 GROUP = 8
 KERNEL_BYTES = 105 * 2**19
 SENTINEL = 4.0
+STRIDE = 37
 MESH = pl.DeviceIdType.MESH
 f32, bf16 = jnp.float32, jnp.bfloat16
 
@@ -30,36 +31,6 @@
     return dot(onehot, hi) + dot(onehot, mid) + dot(onehot, lo)
 
 
-def plan(Z, Y):
-    def step(d, other, n):
-        return 0 if 2 * d != n else (1 if other % 2 == 0 else -1)
-
-    ties = {}
-    for dz in range(Z):
-        for dy in range(Y):
-            shift = (step(dz, dy, Z), step(dy, dz, Y))
-            if shift != (0, 0):
-                ties.setdefault(shift, []).append((dz, dy))
-    offsets, batches = [(0, 0)], []
-    for shift in ((1, 1), (1, 0), (0, 1), (-1, 0), (0, -1)):
-        batches.append((len(offsets), len(ties[shift])) + shift)
-        offsets += ties[shift]
-    seen, runs = set(offsets), []
-    for dz in range(Z):
-        for dy in range(Y):
-            run, a, b = [], dz, dy
-            for _ in range(4):
-                if (a, b) not in seen:
-                    seen.add((a, b))
-                    run.append((a, b))
-                a, b = -b % Z, a
-            if run:
-                runs.append(run)
-    runs.sort(key=lambda run: -sum(min(d, Z - d) for d in run[0]))
-    rest = [o for run in runs for o in run]
-    return offsets + rest, batches
-
-
 def iota(shape, axis):
     return lax.broadcasted_iota(jnp.int32, shape, axis)
 
@@ -81,10 +52,10 @@
     return jnp.sum(jnp.where(earlier, 1.0, 0.0), axis=0, keepdims=True).astype(jnp.int32)
 
 
-def exchange(dims, emb_hbm, lab_hbm, frow, fpart, ans,
-             emb, lab, send, stage, out, recv, other, khi, klo, qht, qlt, bias,
+def exchange(dims, emb_hbm, lab_hbm, slab, frow, fpart, ans,
+             emb, lab, send, recv, other, khi, klo, qht, qlt, bias,
              abuf, ay, ab, az,
-             line_sem, plane_sem, load, gs, gr, fs, fr, ps, pr,
+             line_sem, plane_sem, load, fs, fr, ps, pr,
              nys, nyr, nzs, nzr, nxs, nxr, ncs, ncr, ays, ayr, azs, azr, axs, axr):
     Z, Y, X = dims
     nyz = Z * Y
@@ -95,8 +66,7 @@
     half_t = tiles // 2
     msg = 2 * tiles
     own = 2 * chips
-    offsets, batches = plan(Z, Y)
-    tied = sum(n for _, n, _, _ in batches) + 1
+    back = pow(STRIDE, -1, nyz)
 
     loads = [pltpu.make_async_copy(lab_hbm, lab, load.at[0])]
     part = rows // 4
@@ -142,19 +112,8 @@
     lrow = lab[...]
     rank = ranks(lrow)
     lx, lyz = lrow // nyz, lrow % nyz
-    dx_row = (lx + X - x) % X
     code = ((lyz // Y + Z - z) % Z) * Y + (lyz % Y + Y - y) % Y
-    first_slot = jnp.zeros((1, rows), jnp.int32)
-    per_dx = jnp.ones((1, rows), jnp.int32)
-    for q, (dz, dy) in enumerate(offsets):
-        if q == 0 or q >= tied:
-            first_slot = jnp.where(code == dz * Y + dy, q * X, first_slot)
-    for q0, n, _, _ in batches:
-        for q in range(q0, q0 + n):
-            here = code == offsets[q][0] * Y + offsets[q][1]
-            first_slot = jnp.where(here, q0 * X + q - q0, first_slot)
-            per_dx = jnp.where(here, n, per_dx)
-    target = 2 * (first_slot + dx_row * per_dx) + rank
+    target = 2 * (((code * back) % nyz) * X + (lx + X - x) % X) + rank
 
     pl.semaphore_wait(barrier, Z + Y + X - 2)
     for d in range(1, Y):
@@ -182,47 +141,31 @@
                 slots[:, t * 128:(t + 1) * 128])
 
     def straight(q, dx):
+        w = (q * STRIDE) % nyz
+        where = (((z + w // Y) % Z * Y + (y + w % Y) % Y) * 2 + core, (x + dx) % X)
         piece = pl.ds((q * X + dx) * msg, msg)
-        start(send.at[piece], recv.at[piece], fs, fr.at[q // GROUP], at(*offsets[q], dx))
-
-    def straight_all(i):
-        def step(dx, carry):
-            for q in range(i * chunk_q, (i + 1) * chunk_q):
+        start(send.at[piece], recv.at[piece], fs, fr.at[q // GROUP], where)
+
+    def straight_all(first, last, dxs):
+        def step(q, carry):
+            for dx in dxs:
                 straight(q, dx)
             return carry
-        lax.fori_loop(1, X, step, 0)
-
-    fill(1)
+        lax.fori_loop(first, last, step, 0)
+
+    fill(0)
     pl.semaphore_wait(line_sem, Y - 1)
     for d in range(1, X):
         signal(plane_sem, at(0, 0, d))
-    for q in range(chunk_q, 2 * chunk_q):
-        straight(q, 0)
-    fill(0)
+    straight_all(1, chunk_q, [0])
+    recv[0:msg, :] = send[0:msg, :]
+    fill(1)
     pl.semaphore_wait(plane_sem, X - 1)
-    for b, (q0, n, sz, sy) in enumerate(batches):
-        for dx in range(X):
-            piece = pl.ds((q0 * X + dx * n) * msg, n * msg)
-            start(send.at[piece], stage.at[piece], gs, gr.at[b], at(sz, sy, dx))
-    for dx in range(1, X):
-        straight(0, dx)
-    recv[0:msg, :] = send[0:msg, :]
-    straight_all(1)
-    for b, (q0, n, sz, sy) in enumerate(batches):
-        wait_rows(stage, q0 * X * msg, X * n * msg, gr.at[b])
-        for q in range(q0, q0 + n):
-            for dx in range(X):
-                piece = stage[pl.ds((q0 * X + dx * n + q - q0) * msg, msg), :]
-                out[pl.ds((q * X + dx) * msg, msg), :] = piece
-        for q in range(q0, q0 + n):
-            piece = pl.ds(q * X * msg, X * msg)
-            start(out.at[piece], recv.at[piece], fs, fr.at[q // GROUP],
-                  at(offsets[q][0] - sz, offsets[q][1] - sy))
-    for i in range(2, n_chunk):
-        fill(i)
-        for q in range(i * chunk_q, (i + 1) * chunk_q):
-            straight(q, 0)
-        straight_all(i)
+    straight_all(0, chunk_q, range(1, X))
+    for i in range(1, n_chunk):
+        if i > 1:
+            fill(i)
+        straight_all(i * chunk_q, (i + 1) * chunk_q, range(X))
 
     grows = GROUP * X * msg
     krows = GROUP * X * 2
@@ -250,20 +193,14 @@
 
     mine = jnp.zeros((1, width), f32)
     theirs = jnp.zeros((1, width), f32)
-    per_chunk = n_group // n_chunk
-    order = [g for i in [1, 0] + list(range(2, n_chunk))
-             for g in range(i * per_chunk, (i + 1) * per_chunk)]
-    done = set()
-    for g in order:
+    for g in range(n_group):
         missing = msg if g == 0 else 0
         wait_rows(recv, g * grows + missing, grows - missing, fr.at[g])
         piece = pl.ds(g * grows, grows)
         start(recv.at[piece], other.at[piece], ps, pr.at[g], partner)
         mine = take(recv, g, 0, mine)
-        done.add(g)
         block = g * krows // 128
-        members = [h for h in range(n_group) if h * krows // 128 == block]
-        if done.issuperset(members):
+        if g == n_group - 1 or (g + 1) * krows // 128 > block:
             top = pl.ds(block * 128, min(128, own))
             for t in range(tiles):
                 lanes = pl.ds(t * 128, 128)
@@ -317,7 +254,8 @@
     spread = jnp.where(j == lane_of, best, jnp.where(j == lane_of + 1, cos, 0.0))
     spread = spread.T.reshape(n_group, 2 * X, GROUP, 128)
     spread = jnp.sum(spread, axis=1).reshape(nyz, 128)
-    for q, (dz, dy) in enumerate(offsets):
+    for q in range(nyz):
+        dz, dy = (q * STRIDE) % nyz // Y, (q * STRIDE) % nyz % Y
         abuf[dy * Z + dz:dy * Z + dz + 1, :] = spread[q:q + 1, :]
     for d in range(1, Y):
         start(abuf.at[pl.ds(d * Z, Z)], ay.at[pl.ds(y * Z, Z)], ays, ayr, at(0, -d))
@@ -387,7 +325,6 @@
         wait_rows(fpart, ((x + dx) % X) * xrows, xrows, ncr.at[dx])
     wait_rows(ans, 0, (X - 1) * 8, axr)
 
-    wait_rows(send, 0, (tied - 1) * X * msg, gs)
     wait_rows(send, 0, (chips - 1) * msg, fs)
     wait_rows(recv, 0, n_group * grows, ps)
     wait_rows(frow, 0, (Y - 1) * half_t, nys)
@@ -449,7 +386,6 @@
     rows, width = embeddings.shape
     tiles = width // 128
     n_group = nyz // GROUP
-    n_batch = len(plan(Z, Y)[1])
     linear = 2 * chips * tiles
     half = chips * tiles // 2
     dma = pltpu.SemaphoreType.DMA
@@ -458,6 +394,7 @@
     shape = jax.ShapeDtypeStruct
     regular = pltpu.SemaphoreType.REGULAR
     labels = assignment.reshape(1, rows)
+    slabs = slab_ids.reshape(1, chips)
 
     given = pl.pallas_call(
         functools.partial(exchange, dims),
@@ -466,13 +403,11 @@
             shape((half, 128), f32),
             shape((8 * X, 128), f32),
         ),
-        in_specs=[hbm] * 2,
+        in_specs=[hbm] * 2 + [vmem],
         out_specs=(vmem,) * 3,
         scratch_shapes=[
             pltpu.VMEM((rows, width), f32),
             pltpu.VMEM((1, rows), jnp.int32),
-            pltpu.VMEM((linear, 128), f32),
-            pltpu.VMEM((linear, 128), f32),
             pltpu.VMEM((linear, 128), f32),
             pltpu.VMEM((linear, 128), f32),
             pltpu.VMEM((linear, 128), f32),
@@ -486,14 +421,14 @@
             pltpu.VMEM((nyz, 128), f32),
             pltpu.VMEM((nyz, 128), f32),
             regular, regular,
-            dma((5,)), dma, dma((n_batch,)),
+            dma((5,)),
             dma, dma((n_group,)), dma, dma((n_group,)),
             dma, dma, dma, dma, dma, dma((6,)), dma, dma((X,)),
             dma, dma, dma, dma, dma, dma,
         ],
         compiler_params=pltpu.CompilerParams(
             collective_id=0, has_side_effects=True, vmem_limit_bytes=KERNEL_BYTES),
-    )(embeddings, labels)
+    )(embeddings, labels, slabs)
 
     table, cos, sim = pl.pallas_call(
         functools.partial(finish, dims),
@@ -511,7 +446,7 @@
             dma((6,)),
         ],
         compiler_params=pltpu.CompilerParams(vmem_limit_bytes=32 * 2**20),
-    )(*given, labels, slab_ids.reshape(1, chips), centroids)
+    )(*given, labels, slabs, centroids)
     return table, cos.reshape(rows), sim.reshape(rows)
 
 

time: 90.6 us -> 81.5 us (0.90); the launches traced: 89.1 us -> 80.9 us
  Pallas kernels: 87.1 us -> 79.6 us
    pallas_call x1, Pallas kernels: 85.8 us -> 78.3 us  [local(): pl.pallas_call(functools.partial(exchange, dims), out_shape=(shape((half,...]
where the time goes in v4:
time: 81.5 us; the launch traced here: 80.9 us
  Pallas kernels  79.6 us (98%)
    pallas_call x1, Pallas kernels, local(): pl.pallas_call(functools.partial(exchange, dims), out_shape=(shape((half,...  78.3 us

profile of v4, /device:TPU:1, one launch (start us, length us, event | category | flops | bytes accessed | tf_op | source)
XLA Modules:
  0.0 80.9 jit_solution(6000057791147487489)
XLA Ops:
  0.6 0.0 copy-start.2
  0.6 0.0 copy-start.1
  0.7 0.7 copy-done.2
  1.3 0.0 copy-done.1
  1.3 0.0 copy-start
  1.3 78.3 %shard_map.67 = (f32[768,128]{1,0:T(8,128)S(1)}, f32[768,128]{1,0:T(8,128)S(1)}, f32[32,128]{1,0:T(8,128)S(1)}) custom-call(f32[256,768]{1,0:T(8,128)} %emb_hbm.1, s32[1,256]{1,0:T(1,128)S(1)} %bitcast.4, s32[1,256]{1,0:T(1,128)S(1)} %bitcast.6), custom_call_target="tpu_custom_call" | custom-call | tf_op jit(solution)/shard_map/pallas_call | solution.py:399
  79.6 0.0 copy-done
  79.6 1.3 %shard_map.68 = (f32[128,768]{1,0:T(8,128)}, f32[1,256]{1,0:T(1,128)}, f32[1,256]{1,0:T(1,128)}) custom-call(f32[768,128]{1,0:T(8,128)S(1)} %get-tuple-element.9.frow, f32[768,128]{1,0:T(8,128)S(1)} %get-tuple-element.10.fpart, f32[32,128]{1,0:T(8,128)S(1)} %get-tuple-element.11.ans, s32[1,256]{1,0:T(1,128)S(1)} %bitcast.5, s32[1,256]{1,0:T(1,128)S(1)} %bitcast.7, ...), custom_call_target="tpu_custom_call" | custom-call | tf_op jit(solution)/shard_map/pallas_call | solution.py:433
Async XLA Ops:
  0.6 0.7 copy-start.2
  0.6 0.7 copy-start.1
  1.3 78.3 %copy-start = (f32[128,768]{1,0:T(8,128)S(1)}, f32[128,768]{1,0:T(8,128)}, u32[]{:S(2)}) copy-start(f32[128,768]{1,0:T(8,128)} %cent.1) | copy-start | bytes 1179652

commit v5 on v4

--- a/solution.py
+++ b/solution.py
@@ -53,9 +53,9 @@
 
 
 def exchange(dims, emb_hbm, lab_hbm, slab, frow, fpart, ans,
-             emb, lab, send, recv, other, khi, klo, qht, qlt, bias,
+             emb, lab, send, stage, out, recv, other, keys, queries, bias,
              abuf, ay, ab, az,
-             line_sem, plane_sem, load, fs, fr, ps, pr,
+             line_sem, load, gs, gr, fs, fr, ps, pr,
              nys, nyr, nzs, nzr, nxs, nxr, ncs, ncr, ays, ayr, azs, azr, axs, axr):
     Z, Y, X = dims
     nyz = Z * Y
@@ -113,7 +113,8 @@
     rank = ranks(lrow)
     lx, lyz = lrow // nyz, lrow % nyz
     code = ((lyz // Y + Z - z) % Z) * Y + (lyz % Y + Y - y) % Y
-    target = 2 * (((code * back) % nyz) * X + (lx + X - x) % X) + rank
+    q_row = (code * back) % nyz
+    target = 2 * (((q_row // GROUP) * X + (lx + X - x) % X) * GROUP + q_row % GROUP) + rank
 
     pl.semaphore_wait(barrier, Z + Y + X - 2)
     for d in range(1, Y):
@@ -140,32 +141,42 @@
             send[pl.ds(low * tiles + t, chunk, stride=tiles), :] = (
                 slots[:, t * 128:(t + 1) * 128])
 
-    def straight(q, dx):
+    def owner_at(q):
         w = (q * STRIDE) % nyz
-        where = (((z + w // Y) % Z * Y + (y + w % Y) % Y) * 2 + core, (x + dx) % X)
-        piece = pl.ds((q * X + dx) * msg, msg)
-        start(send.at[piece], recv.at[piece], fs, fr.at[q // GROUP], where)
-
-    def straight_all(first, last, dxs):
-        def step(q, carry):
-            for dx in dxs:
-                straight(q, dx)
-            return carry
-        lax.fori_loop(first, last, step, 0)
-
-    fill(0)
-    pl.semaphore_wait(line_sem, Y - 1)
-    for d in range(1, X):
-        signal(plane_sem, at(0, 0, d))
-    straight_all(1, chunk_q, [0])
-    recv[0:msg, :] = send[0:msg, :]
-    fill(1)
-    pl.semaphore_wait(plane_sem, X - 1)
-    straight_all(0, chunk_q, range(1, X))
-    for i in range(1, n_chunk):
-        if i > 1:
-            fill(i)
-        straight_all(i * chunk_q, (i + 1) * chunk_q, range(X))
+        return ((z + w // Y) % Z * Y + (y + w % Y) % Y) * 2 + core, x
+
+    def straight(q, carry):
+        slot = (q // GROUP * X) * GROUP + q % GROUP
+        start(send.at[pl.ds(slot * msg, msg)], recv.at[pl.ds(q * X * msg, msg)],
+              fs, fr.at[q // GROUP], owner_at(q))
+        return carry
+
+    def onward(q, carry):
+        piece = pl.ds((q * X + 1) * msg, (X - 1) * msg)
+        start(out.at[piece], recv.at[piece], fs, fr.at[q // GROUP], owner_at(q))
+        return carry
+
+    block = GROUP * msg
+    for i in range(n_chunk):
+        fill(i)
+        for g in range(i * chunk_q // GROUP, (i + 1) * chunk_q // GROUP):
+            for dx in range(1, X):
+                start(send.at[pl.ds((g * X + dx) * block, block)],
+                      stage.at[pl.ds((g * (X - 1) + dx - 1) * block, block)],
+                      gs, gr.at[g], at(0, 0, dx))
+        if i == 0:
+            pl.semaphore_wait(line_sem, Y - 1)
+            recv[0:msg, :] = send[0:msg, :]
+        lax.fori_loop(max(i * chunk_q, 1), (i + 1) * chunk_q, straight, 0)
+    for g in range(n_group):
+        wait_rows(stage, g * (X - 1) * block, (X - 1) * block, gr.at[g])
+        for j in range(GROUP):
+            q = g * GROUP + j
+            into = recv if q == 0 else out
+            for dx in range(1, X):
+                into[pl.ds((q * X + dx) * msg, msg), :] = (
+                    stage[pl.ds((g * (X - 1) + dx - 1) * block + j * msg, msg), :])
+        lax.fori_loop(max(g * GROUP, 1), (g + 1) * GROUP, onward, 0)
 
     grows = GROUP * X * msg
     krows = GROUP * X * 2
@@ -186,26 +197,27 @@
             v = jnp.where(dead, 0.0, v)
             hi = v.astype(bf16)
             lo = (v - hi.astype(f32)).astype(bf16)
-            khi[pl.ds(base + g * krows, krows), t * 128:(t + 1) * 128] = hi
-            klo[pl.ds(base + g * krows, krows), t * 128:(t + 1) * 128] = lo
+            for i, v_part in enumerate((hi, lo, hi)):
+                keys[pl.ds(base + g * krows, krows), pl.ds(i * width + t * 128, 128)] = v_part
             columns.append(jnp.sum(v, axis=0, keepdims=True))
         return total + jnp.concatenate(columns, axis=1)
 
     mine = jnp.zeros((1, width), f32)
     theirs = jnp.zeros((1, width), f32)
     for g in range(n_group):
-        missing = msg if g == 0 else 0
+        missing = X * msg if g == 0 else 0
         wait_rows(recv, g * grows + missing, grows - missing, fr.at[g])
         piece = pl.ds(g * grows, grows)
         start(recv.at[piece], other.at[piece], ps, pr.at[g], partner)
         mine = take(recv, g, 0, mine)
-        block = g * krows // 128
-        if g == n_group - 1 or (g + 1) * krows // 128 > block:
-            top = pl.ds(block * 128, min(128, own))
+        tile = g * krows // 128
+        if g == n_group - 1 or (g + 1) * krows // 128 > tile:
+            top = pl.ds(tile * 128, min(128, own))
             for t in range(tiles):
-                lanes = pl.ds(t * 128, 128)
-                qht[lanes, top] = khi[top, lanes].astype(f32).T.astype(bf16)
-                qlt[lanes, top] = klo[top, lanes].astype(f32).T.astype(bf16)
+                hi = keys[top, pl.ds(t * 128, 128)].astype(f32).T.astype(bf16)
+                lo = keys[top, pl.ds(width + t * 128, 128)].astype(f32).T.astype(bf16)
+                for i, v_part in enumerate((hi, hi, lo)):
+                    queries[pl.ds(i * width + t * 128, 128), top] = v_part
         wait_rows(other, g * grows, grows, pr.at[g])
         theirs = take(other, g, own, theirs)
 
@@ -219,24 +231,41 @@
     for d in range(1, Y):
         start(frow.at[piece], frow.at[piece], nys, nyr, at(0, d))
     fh = fresh.astype(bf16)
-    khi[2 * own:2 * own + 16, :] = jnp.broadcast_to(fresh, (16, width)).astype(bf16)
-    klo[2 * own:2 * own + 16, :] = jnp.broadcast_to(
-        fresh - fh.astype(f32), (16, width)).astype(bf16)
+    fl = jnp.broadcast_to(fresh - fh.astype(f32), (16, width)).astype(bf16)
+    fh = jnp.broadcast_to(fresh, (16, width)).astype(bf16)
+    keys[2 * own:2 * own + 16, :] = jnp.concatenate([fh, fl, fh], axis=1)
+
+    xrows = nyz * half_t
+    hrows = xrows // 2
+
+    def block_of(dx, half):
+        return pl.ds(((x + dx) % X) * xrows + half * hrows, hrows)
+
+    def along(dx, half, sem, to):
+        piece = block_of(dx, half)
+        start(frow.at[piece], frow.at[piece], nxs, nxr.at[sem], at(0, 0, to))
+
+    def pass_on(dx):
+        piece = pl.ds(((x + dx) % X) * xrows, xrows)
+        start(frow.at[piece], fpart.at[piece], ncs, ncr.at[dx], partner)
+
+    def landed(dx, half, sem):
+        wait_rows(frow, ((x + dx) % X) * xrows + half * hrows, hrows, nxr.at[sem])
+
+    quarter = own // 2
 
     def product(first, count):
-        kh = khi[first:first + count, :]
-        kl = klo[first:first + count, :]
-        dot = functools.partial(jnp.dot, preferred_element_type=f32)
-        return dot(kh, qht[...]) + dot(kh, qlt[...]) + dot(kl, qht[...])
+        return jnp.dot(keys[first:first + count, :], queries[...], preferred_element_type=f32)
 
     def closest(s, first):
-        off = bias[first:first + own, :]
+        off = bias[first:first + quarter, :]
         s = s + (jnp.concatenate([off] * (own // 128), axis=1) if own > 128 else off[:, :own])
-        if first == 0:
-            s = jnp.where(iota((own, own), 0) == iota((own, own), 1), -4.0, s)
+        if first < own:
+            itself = iota((quarter, own), 0) + first == iota((quarter, own), 1)
+            s = jnp.where(itself, -4.0, s)
         return jnp.max(s, axis=0, keepdims=True)
 
-    best = jnp.maximum(closest(product(0, own), 0), -1.0)
+    best = jnp.maximum(closest(product(0, quarter), 0), -1.0)
 
     yrows = Y * half_t
     wait_rows(frow, 0, (Y - 1) * half_t, nyr)
@@ -244,9 +273,21 @@
     for d in range(1, Z):
         start(frow.at[piece], frow.at[piece], nzs, nzr, at(d, 0))
 
-    s = product(own, own + 16)
-    best = jnp.maximum(best, closest(s[:own, :], own))
-    cos = s[own:own + 1, :]
+    best = jnp.maximum(best, closest(product(quarter, quarter), quarter))
+    best = jnp.maximum(best, closest(product(own, quarter), own))
+
+    wait_rows(frow, 0, (Z - 1) * yrows, nzr)
+    along(0, 0, 0, 1)
+    if X > 2:
+        along(0, 1, 2, X - 1)
+    along(0, 1, 1, 1)
+    if X > 2:
+        along(0, 0, 3, X - 1)
+    pass_on(0)
+
+    s = product(own + quarter, quarter + 16)
+    best = jnp.maximum(best, closest(s[:quarter, :], own + quarter))
+    cos = s[quarter:quarter + 1, :]
 
     xs = (iota((128, own), 1) // GROUP) % (2 * X)
     lane_of = (xs // 2) * 8 + (xs % 2) * 2
@@ -261,31 +302,6 @@
         start(abuf.at[pl.ds(d * Z, Z)], ay.at[pl.ds(y * Z, Z)], ays, ayr, at(0, -d))
     ay[pl.ds(y * Z, Z), :] = abuf[0:Z, :]
 
-    xrows = nyz * half_t
-    hrows = xrows // 2
-
-    def block_of(dx, half):
-        return pl.ds(((x + dx) % X) * xrows + half * hrows, hrows)
-
-    def along(dx, half, sem, to):
-        piece = block_of(dx, half)
-        start(frow.at[piece], frow.at[piece], nxs, nxr.at[sem], at(0, 0, to))
-
-    def pass_on(dx):
-        piece = pl.ds(((x + dx) % X) * xrows, xrows)
-        start(frow.at[piece], fpart.at[piece], ncs, ncr.at[dx], partner)
-
-    def landed(dx, half, sem):
-        wait_rows(frow, ((x + dx) % X) * xrows + half * hrows, hrows, nxr.at[sem])
-
-    wait_rows(frow, 0, (Z - 1) * yrows, nzr)
-    along(0, 0, 0, 1)
-    if X > 2:
-        along(0, 1, 2, X - 1)
-    along(0, 1, 1, 1)
-    if X > 2:
-        along(0, 0, 3, X - 1)
-    pass_on(0)
     if X > 2:
         landed(X - 1, 0, 0)
         along(X - 1, 0, 4, 1)
@@ -325,7 +341,8 @@
         wait_rows(fpart, ((x + dx) % X) * xrows, xrows, ncr.at[dx])
     wait_rows(ans, 0, (X - 1) * 8, axr)
 
-    wait_rows(send, 0, (chips - 1) * msg, fs)
+    wait_rows(send, 0, (X - 1) * nyz * msg, gs)
+    wait_rows(send, 0, (nyz - 1) * X * msg, fs)
     wait_rows(recv, 0, n_group * grows, ps)
     wait_rows(frow, 0, (Y - 1) * half_t, nys)
     wait_rows(frow, 0, (Z - 1) * yrows, nzs)
@@ -409,19 +426,19 @@
             pltpu.VMEM((rows, width), f32),
             pltpu.VMEM((1, rows), jnp.int32),
             pltpu.VMEM((linear, 128), f32),
+            pltpu.VMEM((linear // X * (X - 1), 128), f32),
             pltpu.VMEM((linear, 128), f32),
             pltpu.VMEM((linear, 128), f32),
-            pltpu.VMEM((4 * chips + 16, width), bf16),
-            pltpu.VMEM((4 * chips + 16, width), bf16),
-            pltpu.VMEM((width, 2 * chips), bf16),
-            pltpu.VMEM((width, 2 * chips), bf16),
+            pltpu.VMEM((linear, 128), f32),
+            pltpu.VMEM((4 * chips + 16, 3 * width), bf16),
+            pltpu.VMEM((3 * width, 2 * chips), bf16),
             pltpu.VMEM((4 * chips, 128), f32),
             pltpu.VMEM((max(nyz, 8 * X), 128), f32),
             pltpu.VMEM((nyz, 128), f32),
             pltpu.VMEM((nyz, 128), f32),
             pltpu.VMEM((nyz, 128), f32),
-            regular, regular,
-            dma((5,)),
+            regular,
+            dma((5,)), dma, dma((n_group,)),
             dma, dma((n_group,)), dma, dma((n_group,)),
             dma, dma, dma, dma, dma, dma((6,)), dma, dma((X,)),
             dma, dma, dma, dma, dma, dma,

time: 81.5 us -> 82.8 us (1.016); the launches traced: 80.9 us -> 81.2 us
  no operation moved by 1% of the time
where the time goes in v5:
time: 82.8 us; the launch traced here: 81.2 us
  Pallas kernels  79.9 us (96%)
    pallas_call x1, Pallas kernels, local(): pl.pallas_call(functools.partial(exchange, dims), out_shape=(shape((half,...  78.5 us

profile of v5, /device:TPU:1, one launch (start us, length us, event | category | flops | bytes accessed | tf_op | source)
XLA Modules:
  0.0 81.2 jit_solution(18111371113655547498)
XLA Ops:
  0.6 0.0 copy-start.2
  0.6 0.0 copy-start.1
  0.7 0.7 copy-done.2
  1.3 0.0 copy-done.1
  1.3 0.0 copy-start
  1.3 78.5 %shard_map.67 = (f32[768,128]{1,0:T(8,128)S(1)}, f32[768,128]{1,0:T(8,128)S(1)}, f32[32,128]{1,0:T(8,128)S(1)}) custom-call(f32[256,768]{1,0:T(8,128)} %emb_hbm.1, s32[1,256]{1,0:T(1,128)S(1)} %bitcast.4, s32[1,256]{1,0:T(1,128)S(1)} %bitcast.6), custom_call_target="tpu_custom_call" | custom-call | tf_op jit(solution)/shard_map/pallas_call | solution.py:416
  79.9 0.0 copy-done
  79.9 1.3 %shard_map.68 = (f32[128,768]{1,0:T(8,128)}, f32[1,256]{1,0:T(1,128)}, f32[1,256]{1,0:T(1,128)}) custom-call(f32[768,128]{1,0:T(8,128)S(1)} %get-tuple-element.9.frow, f32[768,128]{1,0:T(8,128)S(1)} %get-tuple-element.10.fpart, f32[32,128]{1,0:T(8,128)S(1)} %get-tuple-element.11.ans, s32[1,256]{1,0:T(1,128)S(1)} %bitcast.5, s32[1,256]{1,0:T(1,128)S(1)} %bitcast.7, ...), custom_call_target="tpu_custom_call" | custom-call | tf_op jit(solution)/shard_map/pallas_call | solution.py:450
Async XLA Ops:
  0.6 0.7 copy-start.2
  0.6 0.7 copy-start.1
  1.3 78.6 %copy-start = (f32[128,768]{1,0:T(8,128)S(1)}, f32[128,768]{1,0:T(8,128)}, u32[]{:S(2)}) copy-start(f32[128,768]{1,0:T(8,128)} %cent.1) | copy-start | bytes 1179652

commit v6 on v4

--- a/solution.py
+++ b/solution.py
@@ -53,9 +53,9 @@
 
 
 def exchange(dims, emb_hbm, lab_hbm, slab, frow, fpart, ans,
-             emb, lab, send, recv, other, khi, klo, qht, qlt, bias,
+             emb, lab, send, recv, other, keys, queries, bias, part_sum,
              abuf, ay, ab, az,
-             line_sem, plane_sem, load, fs, fr, ps, pr,
+             line_sem, plane_sem, load, fs, fr, ps, pr, ss, sr,
              nys, nyr, nzs, nzr, nxs, nxr, ncs, ncr, ays, ayr, azs, azr, axs, axr):
     Z, Y, X = dims
     nyz = Z * Y
@@ -186,30 +186,62 @@
             v = jnp.where(dead, 0.0, v)
             hi = v.astype(bf16)
             lo = (v - hi.astype(f32)).astype(bf16)
-            khi[pl.ds(base + g * krows, krows), t * 128:(t + 1) * 128] = hi
-            klo[pl.ds(base + g * krows, krows), t * 128:(t + 1) * 128] = lo
+            for i, v_part in enumerate((hi, lo, hi)):
+                keys[pl.ds(base + g * krows, krows), pl.ds(i * width + t * 128, 128)] = v_part
             columns.append(jnp.sum(v, axis=0, keepdims=True))
         return total + jnp.concatenate(columns, axis=1)
 
+    half = own // 2
+
+    def product(first, count, side):
+        return jnp.dot(keys[first:first + count, :], queries[:, side * half:(side + 1) * half],
+                       preferred_element_type=f32)
+
+    def closest(s, first, side):
+        count = s.shape[0]
+        off = bias[first:first + count, :]
+        s = s + (jnp.concatenate([off] * (half // 128), axis=1) if half > 128 else off[:, :half])
+        if first < own:
+            itself = iota((count, half), 0) + first == iota((count, half), 1) + side * half
+            s = jnp.where(itself, -4.0, s)
+        return jnp.max(s, axis=0, keepdims=True)
+
+    best = [jnp.full((1, half), -1.0, f32)] * 2
+
+    def compare(first, count, side):
+        best[side] = jnp.maximum(best[side], closest(product(first, count, side), first, side))
+
     mine = jnp.zeros((1, width), f32)
-    theirs = jnp.zeros((1, width), f32)
     for g in range(n_group):
         missing = msg if g == 0 else 0
         wait_rows(recv, g * grows + missing, grows - missing, fr.at[g])
         piece = pl.ds(g * grows, grows)
         start(recv.at[piece], other.at[piece], ps, pr.at[g], partner)
         mine = take(recv, g, 0, mine)
-        block = g * krows // 128
-        if g == n_group - 1 or (g + 1) * krows // 128 > block:
-            top = pl.ds(block * 128, min(128, own))
+        have = (g + 1) * krows
+        turn = 128 if half % 128 == 0 else krows
+        if have % turn == 0:
+            top = pl.ds(have - turn, turn)
             for t in range(tiles):
-                lanes = pl.ds(t * 128, 128)
-                qht[lanes, top] = khi[top, lanes].astype(f32).T.astype(bf16)
-                qlt[lanes, top] = klo[top, lanes].astype(f32).T.astype(bf16)
+                hi = keys[top, pl.ds(t * 128, 128)].astype(f32).T.astype(bf16)
+                lo = keys[top, pl.ds(width + t * 128, 128)].astype(f32).T.astype(bf16)
+                for i, v_part in enumerate((hi, hi, lo)):
+                    queries[pl.ds(i * width + t * 128, 128), top] = v_part
+        if g == n_group - 1:
+            part_sum[0] = mine
+            start(part_sum.at[0], part_sum.at[1], ss, sr, partner)
+            break
         wait_rows(other, g * grows, grows, pr.at[g])
-        theirs = take(other, g, own, theirs)
-
-    sums = mine + theirs
+        take(other, g, own, mine)
+        if have == half:
+            seen = 0
+        if have == half or (have > half and (have - half) % 128 == 0):
+            compare(seen, have - seen, 0)
+            compare(own + seen, have - seen, 0)
+            seen = have
+
+    wait_rows(part_sum, 1, 1, sr)
+    sums = mine + part_sum[1]
     fresh = sums * lax.rsqrt(jnp.sum(sums * sums, axis=1, keepdims=True) + epsilon)
     for t in range(half_t):
         a = fresh[:, t * 128:(t + 1) * 128]
@@ -219,24 +251,31 @@
     for d in range(1, Y):
         start(frow.at[piece], frow.at[piece], nys, nyr, at(0, d))
     fh = fresh.astype(bf16)
-    khi[2 * own:2 * own + 16, :] = jnp.broadcast_to(fresh, (16, width)).astype(bf16)
-    klo[2 * own:2 * own + 16, :] = jnp.broadcast_to(
-        fresh - fh.astype(f32), (16, width)).astype(bf16)
-
-    def product(first, count):
-        kh = khi[first:first + count, :]
-        kl = klo[first:first + count, :]
-        dot = functools.partial(jnp.dot, preferred_element_type=f32)
-        return dot(kh, qht[...]) + dot(kh, qlt[...]) + dot(kl, qht[...])
-
-    def closest(s, first):
-        off = bias[first:first + own, :]
-        s = s + (jnp.concatenate([off] * (own // 128), axis=1) if own > 128 else off[:, :own])
-        if first == 0:
-            s = jnp.where(iota((own, own), 0) == iota((own, own), 1), -4.0, s)
-        return jnp.max(s, axis=0, keepdims=True)
-
-    best = jnp.maximum(closest(product(0, own), 0), -1.0)
+    fl = jnp.broadcast_to(fresh - fh.astype(f32), (16, width)).astype(bf16)
+    fh = jnp.broadcast_to(fresh, (16, width)).astype(bf16)
+    keys[2 * own:2 * own + 16, :] = jnp.concatenate([fh, fl, fh], axis=1)
+
+    xrows = nyz * half_t
+    hrows = xrows // 2
+
+    def block_of(dx, half):
+        return pl.ds(((x + dx) % X) * xrows + half * hrows, hrows)
+
+    def along(dx, half, sem, to):
+        piece = block_of(dx, half)
+        start(frow.at[piece], frow.at[piece], nxs, nxr.at[sem], at(0, 0, to))
+
+    def pass_on(dx):
+        piece = pl.ds(((x + dx) % X) * xrows, xrows)
+        start(frow.at[piece], fpart.at[piece], ncs, ncr.at[dx], partner)
+
+    def landed(dx, half, sem):
+        wait_rows(frow, ((x + dx) % X) * xrows + half * hrows, hrows, nxr.at[sem])
+
+    wait_rows(other, (n_group - 1) * grows, grows, pr.at[n_group - 1])
+    take(other, n_group - 1, own, mine)
+    compare(0, half, 1)
+    compare(half, half, 1)
 
     yrows = Y * half_t
     wait_rows(frow, 0, (Y - 1) * half_t, nyr)
@@ -244,9 +283,26 @@
     for d in range(1, Z):
         start(frow.at[piece], frow.at[piece], nzs, nzr, at(d, 0))
 
-    s = product(own, own + 16)
-    best = jnp.maximum(best, closest(s[:own, :], own))
-    cos = s[own:own + 1, :]
+    compare(seen, own - seen, 0)
+    compare(own, half, 1)
+
+    wait_rows(frow, 0, (Z - 1) * yrows, nzr)
+    along(0, 0, 0, 1)
+    if X > 2:
+        along(0, 1, 2, X - 1)
+    along(0, 1, 1, 1)
+    if X > 2:
+        along(0, 0, 3, X - 1)
+    pass_on(0)
+
+    cos = []
+    for side, first in ((0, own + seen), (1, own + half)):
+        count = 2 * own - first
+        s = product(first, count + 16, side)
+        best[side] = jnp.maximum(best[side], closest(s[:count, :], first, side))
+        cos.append(s[count:count + 1, :])
+    best = jnp.concatenate(best, axis=1)
+    cos = jnp.concatenate(cos, axis=1)
 
     xs = (iota((128, own), 1) // GROUP) % (2 * X)
     lane_of = (xs // 2) * 8 + (xs % 2) * 2
@@ -261,31 +317,6 @@
         start(abuf.at[pl.ds(d * Z, Z)], ay.at[pl.ds(y * Z, Z)], ays, ayr, at(0, -d))
     ay[pl.ds(y * Z, Z), :] = abuf[0:Z, :]
 
-    xrows = nyz * half_t
-    hrows = xrows // 2
-
-    def block_of(dx, half):
-        return pl.ds(((x + dx) % X) * xrows + half * hrows, hrows)
-
-    def along(dx, half, sem, to):
-        piece = block_of(dx, half)
-        start(frow.at[piece], frow.at[piece], nxs, nxr.at[sem], at(0, 0, to))
-
-    def pass_on(dx):
-        piece = pl.ds(((x + dx) % X) * xrows, xrows)
-        start(frow.at[piece], fpart.at[piece], ncs, ncr.at[dx], partner)
-
-    def landed(dx, half, sem):
-        wait_rows(frow, ((x + dx) % X) * xrows + half * hrows, hrows, nxr.at[sem])
-
-    wait_rows(frow, 0, (Z - 1) * yrows, nzr)
-    along(0, 0, 0, 1)
-    if X > 2:
-        along(0, 1, 2, X - 1)
-    along(0, 1, 1, 1)
-    if X > 2:
-        along(0, 0, 3, X - 1)
-    pass_on(0)
     if X > 2:
         landed(X - 1, 0, 0)
         along(X - 1, 0, 4, 1)
@@ -326,6 +357,7 @@
     wait_rows(ans, 0, (X - 1) * 8, axr)
 
     wait_rows(send, 0, (chips - 1) * msg, fs)
+    wait_rows(part_sum, 0, 1, ss)
     wait_rows(recv, 0, n_group * grows, ps)
     wait_rows(frow, 0, (Y - 1) * half_t, nys)
     wait_rows(frow, 0, (Z - 1) * yrows, nzs)
@@ -411,18 +443,17 @@
             pltpu.VMEM((linear, 128), f32),
             pltpu.VMEM((linear, 128), f32),
             pltpu.VMEM((linear, 128), f32),
-            pltpu.VMEM((4 * chips + 16, width), bf16),
-            pltpu.VMEM((4 * chips + 16, width), bf16),
-            pltpu.VMEM((width, 2 * chips), bf16),
-            pltpu.VMEM((width, 2 * chips), bf16),
+            pltpu.VMEM((4 * chips + 16, 3 * width), bf16),
+            pltpu.VMEM((3 * width, 2 * chips), bf16),
             pltpu.VMEM((4 * chips, 128), f32),
+            pltpu.VMEM((2, 1, width), f32),
             pltpu.VMEM((max(nyz, 8 * X), 128), f32),
             pltpu.VMEM((nyz, 128), f32),
             pltpu.VMEM((nyz, 128), f32),
             pltpu.VMEM((nyz, 128), f32),
             regular, regular,
             dma((5,)),
-            dma, dma((n_group,)), dma, dma((n_group,)),
+            dma, dma((n_group,)), dma, dma((n_group,)), dma, dma,
             dma, dma, dma, dma, dma, dma((6,)), dma, dma((X,)),
             dma, dma, dma, dma, dma, dma,
         ],

time: 81.5 us -> 84.1 us (1.032)
  Pallas kernels: 79.6 us -> 82.6 us
    pallas_call x1, Pallas kernels: 78.3 us -> 81.3 us  [local(): pl.pallas_call(functools.partial(exchange, dims), out_shape=(shape((half,...]
where the time goes in v6:
time: 84.1 us; the launch traced here: 84 us
  Pallas kernels  82.6 us (98%)
    pallas_call x1, Pallas kernels, local(): pl.pallas_call(functools.partial(exchange, dims), out_shape=(shape((half,...  81.3 us

profile of v6, /device:TPU:1, one launch (start us, length us, event | category | flops | bytes accessed | tf_op | source)
XLA Modules:
  0.0 84.0 jit_solution(327519538134887427)
XLA Ops:
  0.6 0.0 copy-start.2
  0.6 0.0 copy-start.1
  0.7 0.7 copy-done.2
  1.3 0.0 copy-done.1
  1.3 0.0 copy-start
  1.3 81.3 %shard_map.67 = (f32[768,128]{1,0:T(8,128)S(1)}, f32[768,128]{1,0:T(8,128)S(1)}, f32[32,128]{1,0:T(8,128)S(1)}) custom-call(f32[256,768]{1,0:T(8,128)} %emb_hbm.1, s32[1,256]{1,0:T(1,128)S(1)} %bitcast.4, s32[1,256]{1,0:T(1,128)S(1)} %bitcast.6), custom_call_target="tpu_custom_call" | custom-call | tf_op jit(solution)/shard_map/pallas_call | solution.py:431
  82.6 0.0 copy-done
  82.6 1.3 %shard_map.68 = (f32[128,768]{1,0:T(8,128)}, f32[1,256]{1,0:T(1,128)}, f32[1,256]{1,0:T(1,128)}) custom-call(f32[768,128]{1,0:T(8,128)S(1)} %get-tuple-element.9.frow, f32[768,128]{1,0:T(8,128)S(1)} %get-tuple-element.10.fpart, f32[32,128]{1,0:T(8,128)S(1)} %get-tuple-element.11.ans, s32[1,256]{1,0:T(1,128)S(1)} %bitcast.5, s32[1,256]{1,0:T(1,128)S(1)} %bitcast.7, ...), custom_call_target="tpu_custom_call" | custom-call | tf_op jit(solution)/shard_map/pallas_call | solution.py:464
Async XLA Ops:
  0.6 0.7 copy-start.2
  0.6 0.7 copy-start.1
  1.3 81.3 %copy-start = (f32[128,768]{1,0:T(8,128)S(1)}, f32[128,768]{1,0:T(8,128)}, u32[]{:S(2)}) copy-start(f32[128,768]{1,0:T(8,128)} %cent.1) | copy-start | bytes 1179652

commit v7 on v4

--- a/solution.py
+++ b/solution.py
@@ -53,9 +53,9 @@
 
 
 def exchange(dims, emb_hbm, lab_hbm, slab, frow, fpart, ans,
-             emb, lab, send, recv, other, khi, klo, qht, qlt, bias,
+             emb, lab, send, recv, other, khi, klo, qht, qlt, bias, part_sum,
              abuf, ay, ab, az,
-             line_sem, plane_sem, load, fs, fr, ps, pr,
+             line_sem, plane_sem, load, fs, fr, ps, pr, ss, sr,
              nys, nyr, nzs, nzr, nxs, nxr, ncs, ncr, ays, ayr, azs, azr, axs, axr):
     Z, Y, X = dims
     nyz = Z * Y
@@ -174,12 +174,7 @@
         columns = []
         dead = None
         for t in range(tiles):
-            pieces = []
-            for dx in range(X):
-                for s in range(2):
-                    first = g * grows + dx * msg + s * tiles + t
-                    pieces.append(buf[pl.ds(first, GROUP, stride=X * msg), :])
-            v = jnp.concatenate(pieces, axis=0)
+            v = buf[pl.ds(g * grows + t, krows, stride=tiles), :]
             if dead is None:
                 dead = v > 2.0
                 bias[pl.ds(base + g * krows, krows), :] = jnp.where(dead, -4.0, 0.0)
@@ -191,25 +186,40 @@
             columns.append(jnp.sum(v, axis=0, keepdims=True))
         return total + jnp.concatenate(columns, axis=1)
 
+    def take_own(g, total):
+        total = take(recv, g, 0, total)
+        have = (g + 1) * krows
+        turn = 128 if own % 128 == 0 else krows
+        if have % turn == 0:
+            top = pl.ds(have - turn, turn)
+            for t in range(tiles):
+                lanes = pl.ds(t * 128, 128)
+                qht[lanes, top] = khi[top, lanes].astype(f32).T.astype(bf16)
+                qlt[lanes, top] = klo[top, lanes].astype(f32).T.astype(bf16)
+        return total
+
+    def take_other(g):
+        wait_rows(other, g * grows, grows, pr.at[g])
+        take(other, g, own, mine)
+
     mine = jnp.zeros((1, width), f32)
-    theirs = jnp.zeros((1, width), f32)
     for g in range(n_group):
         missing = msg if g == 0 else 0
         wait_rows(recv, g * grows + missing, grows - missing, fr.at[g])
         piece = pl.ds(g * grows, grows)
         start(recv.at[piece], other.at[piece], ps, pr.at[g], partner)
-        mine = take(recv, g, 0, mine)
-        block = g * krows // 128
-        if g == n_group - 1 or (g + 1) * krows // 128 > block:
-            top = pl.ds(block * 128, min(128, own))
-            for t in range(tiles):
-                lanes = pl.ds(t * 128, 128)
-                qht[lanes, top] = khi[top, lanes].astype(f32).T.astype(bf16)
-                qlt[lanes, top] = klo[top, lanes].astype(f32).T.astype(bf16)
-        wait_rows(other, g * grows, grows, pr.at[g])
-        theirs = take(other, g, own, theirs)
-
-    sums = mine + theirs
+        if g > 0:
+            mine = take_own(g - 1, mine)
+        if g > 1:
+            take_other(g - 2)
+    mine = take_own(n_group - 1, mine)
+    part_sum[0] = mine
+    start(part_sum.at[0], part_sum.at[1], ss, sr, partner)
+    for g in range(max(n_group - 2, 0), n_group):
+        take_other(g)
+
+    wait_rows(part_sum, 1, 1, sr)
+    sums = mine + part_sum[1]
     fresh = sums * lax.rsqrt(jnp.sum(sums * sums, axis=1, keepdims=True) + epsilon)
     for t in range(half_t):
         a = fresh[:, t * 128:(t + 1) * 128]
@@ -248,12 +258,11 @@
     best = jnp.maximum(best, closest(s[:own, :], own))
     cos = s[own:own + 1, :]
 
-    xs = (iota((128, own), 1) // GROUP) % (2 * X)
+    xs = iota((128, own), 1) % (2 * X)
     lane_of = (xs // 2) * 8 + (xs % 2) * 2
     j = iota((128, own), 0)
     spread = jnp.where(j == lane_of, best, jnp.where(j == lane_of + 1, cos, 0.0))
-    spread = spread.T.reshape(n_group, 2 * X, GROUP, 128)
-    spread = jnp.sum(spread, axis=1).reshape(nyz, 128)
+    spread = jnp.sum(spread.T.reshape(nyz, 2 * X, 128), axis=1)
     for q in range(nyz):
         dz, dy = (q * STRIDE) % nyz // Y, (q * STRIDE) % nyz % Y
         abuf[dy * Z + dz:dy * Z + dz + 1, :] = spread[q:q + 1, :]
@@ -326,6 +335,7 @@
     wait_rows(ans, 0, (X - 1) * 8, axr)
 
     wait_rows(send, 0, (chips - 1) * msg, fs)
+    wait_rows(part_sum, 0, 1, ss)
     wait_rows(recv, 0, n_group * grows, ps)
     wait_rows(frow, 0, (Y - 1) * half_t, nys)
     wait_rows(frow, 0, (Z - 1) * yrows, nzs)
@@ -416,13 +426,14 @@
             pltpu.VMEM((width, 2 * chips), bf16),
             pltpu.VMEM((width, 2 * chips), bf16),
             pltpu.VMEM((4 * chips, 128), f32),
+            pltpu.VMEM((2, 1, width), f32),
             pltpu.VMEM((max(nyz, 8 * X), 128), f32),
             pltpu.VMEM((nyz, 128), f32),
             pltpu.VMEM((nyz, 128), f32),
             pltpu.VMEM((nyz, 128), f32),
             regular, regular,
             dma((5,)),
-            dma, dma((n_group,)), dma, dma((n_group,)),
+            dma, dma((n_group,)), dma, dma((n_group,)), dma, dma,
             dma, dma, dma, dma, dma, dma((6,)), dma, dma((X,)),
             dma, dma, dma, dma, dma, dma,
         ],

time: 81.5 us -> 81.4 us (level)
  no operation moved by 1% of the time
where the time goes in v7:
time: 81.4 us; the launch traced here: 81 us
  Pallas kernels  79.6 us (98%)
    pallas_call x1, Pallas kernels, local(): pl.pallas_call(functools.partial(exchange, dims), out_shape=(shape((half,...  78.3 us

profile of v7, /device:TPU:1, one launch (start us, length us, event | category | flops | bytes accessed | tf_op | source)
XLA Modules:
  0.0 81.0 jit_solution(9131292251654291756)
XLA Ops:
  0.6 0.0 copy-start.2
  0.6 0.0 copy-start.1
  0.7 0.7 copy-done.2
  1.3 0.0 copy-done.1
  1.3 0.0 copy-start
  1.3 78.3 %shard_map.67 = (f32[768,128]{1,0:T(8,128)S(1)}, f32[768,128]{1,0:T(8,128)S(1)}, f32[32,128]{1,0:T(8,128)S(1)}) custom-call(f32[256,768]{1,0:T(8,128)} %emb_hbm.1, s32[1,256]{1,0:T(1,128)S(1)} %bitcast.4, s32[1,256]{1,0:T(1,128)S(1)} %bitcast.6), custom_call_target="tpu_custom_call" | custom-call | tf_op jit(solution)/shard_map/pallas_call | solution.py:409
  79.6 0.0 copy-done
  79.7 1.3 %shard_map.68 = (f32[128,768]{1,0:T(8,128)}, f32[1,256]{1,0:T(1,128)}, f32[1,256]{1,0:T(1,128)}) custom-call(f32[768,128]{1,0:T(8,128)S(1)} %get-tuple-element.9.frow, f32[768,128]{1,0:T(8,128)S(1)} %get-tuple-element.10.fpart, f32[32,128]{1,0:T(8,128)S(1)} %get-tuple-element.11.ans, s32[1,256]{1,0:T(1,128)S(1)} %bitcast.5, s32[1,256]{1,0:T(1,128)S(1)} %bitcast.7, ...), custom_call_target="tpu_custom_call" | custom-call | tf_op jit(solution)/shard_map/pallas_call | solution.py:444
Async XLA Ops:
  0.6 0.7 copy-start.2
  0.6 0.7 copy-start.1
  1.3 78.3 %copy-start = (f32[128,768]{1,0:T(8,128)S(1)}, f32[128,768]{1,0:T(8,128)}, u32[]{:S(2)}) copy-start(f32[128,768]{1,0:T(8,128)} %cent.1) | copy-start | bytes 1179652

commit v8 on v7

--- a/solution.py
+++ b/solution.py
@@ -53,9 +53,9 @@
 
 
 def exchange(dims, emb_hbm, lab_hbm, slab, frow, fpart, ans,
-             emb, lab, send, recv, other, khi, klo, qht, qlt, bias, part_sum,
+             emb, lab, send, stage, out, recv, other, khi, klo, qht, qlt, bias, part_sum,
              abuf, ay, ab, az,
-             line_sem, plane_sem, load, fs, fr, ps, pr, ss, sr,
+             line_sem, load, gs, gr, fs, fr, ps, pr, ss, sr,
              nys, nyr, nzs, nzr, nxs, nxr, ncs, ncr, ays, ayr, azs, azr, axs, axr):
     Z, Y, X = dims
     nyz = Z * Y
@@ -113,7 +113,8 @@
     rank = ranks(lrow)
     lx, lyz = lrow // nyz, lrow % nyz
     code = ((lyz // Y + Z - z) % Z) * Y + (lyz % Y + Y - y) % Y
-    target = 2 * (((code * back) % nyz) * X + (lx + X - x) % X) + rank
+    q_row = (code * back) % nyz
+    target = 2 * (((q_row // GROUP) * X + (lx + X - x) % X) * GROUP + q_row % GROUP) + rank
 
     pl.semaphore_wait(barrier, Z + Y + X - 2)
     for d in range(1, Y):
@@ -140,32 +141,42 @@
             send[pl.ds(low * tiles + t, chunk, stride=tiles), :] = (
                 slots[:, t * 128:(t + 1) * 128])
 
-    def straight(q, dx):
+    def owner_at(q):
         w = (q * STRIDE) % nyz
-        where = (((z + w // Y) % Z * Y + (y + w % Y) % Y) * 2 + core, (x + dx) % X)
-        piece = pl.ds((q * X + dx) * msg, msg)
-        start(send.at[piece], recv.at[piece], fs, fr.at[q // GROUP], where)
-
-    def straight_all(first, last, dxs):
-        def step(q, carry):
-            for dx in dxs:
-                straight(q, dx)
-            return carry
-        lax.fori_loop(first, last, step, 0)
-
-    fill(0)
-    pl.semaphore_wait(line_sem, Y - 1)
-    for d in range(1, X):
-        signal(plane_sem, at(0, 0, d))
-    straight_all(1, chunk_q, [0])
-    recv[0:msg, :] = send[0:msg, :]
-    fill(1)
-    pl.semaphore_wait(plane_sem, X - 1)
-    straight_all(0, chunk_q, range(1, X))
-    for i in range(1, n_chunk):
-        if i > 1:
-            fill(i)
-        straight_all(i * chunk_q, (i + 1) * chunk_q, range(X))
+        return ((z + w // Y) % Z * Y + (y + w % Y) % Y) * 2 + core, x
+
+    def straight(q, carry):
+        slot = (q // GROUP * X) * GROUP + q % GROUP
+        start(send.at[pl.ds(slot * msg, msg)], recv.at[pl.ds(q * X * msg, msg)],
+              fs, fr.at[q // GROUP], owner_at(q))
+        return carry
+
+    def onward(q, carry):
+        piece = pl.ds((q * X + 1) * msg, (X - 1) * msg)
+        start(out.at[piece], recv.at[piece], fs, fr.at[q // GROUP], owner_at(q))
+        return carry
+
+    block = GROUP * msg
+    for i in range(n_chunk):
+        fill(i)
+        for g in range(i * chunk_q // GROUP, (i + 1) * chunk_q // GROUP):
+            for dx in range(1, X):
+                start(send.at[pl.ds((g * X + dx) * block, block)],
+                      stage.at[pl.ds((g * (X - 1) + dx - 1) * block, block)],
+                      gs, gr.at[g], at(0, 0, dx))
+        if i == 0:
+            pl.semaphore_wait(line_sem, Y - 1)
+            recv[0:msg, :] = send[0:msg, :]
+        lax.fori_loop(max(i * chunk_q, 1), (i + 1) * chunk_q, straight, 0)
+    for g in range(n_group):
+        wait_rows(stage, g * (X - 1) * block, (X - 1) * block, gr.at[g])
+        for j in range(GROUP):
+            q = g * GROUP + j
+            into = recv if q == 0 else out
+            for dx in range(1, X):
+                into[pl.ds((q * X + dx) * msg, msg), :] = (
+                    stage[pl.ds((g * (X - 1) + dx - 1) * block + j * msg, msg), :])
+        lax.fori_loop(max(g * GROUP, 1), (g + 1) * GROUP, onward, 0)
 
     grows = GROUP * X * msg
     krows = GROUP * X * 2
@@ -204,7 +215,7 @@
 
     mine = jnp.zeros((1, width), f32)
     for g in range(n_group):
-        missing = msg if g == 0 else 0
+        missing = X * msg if g == 0 else 0
         wait_rows(recv, g * grows + missing, grows - missing, fr.at[g])
         piece = pl.ds(g * grows, grows)
         start(recv.at[piece], other.at[piece], ps, pr.at[g], partner)
@@ -258,6 +269,31 @@
     best = jnp.maximum(best, closest(s[:own, :], own))
     cos = s[own:own + 1, :]
 
+    xrows = nyz * half_t
+    hrows = xrows // 2
+
+    def block_of(dx, half):
+        return pl.ds(((x + dx) % X) * xrows + half * hrows, hrows)
+
+    def along(dx, half, sem, to):
+        piece = block_of(dx, half)
+        start(frow.at[piece], frow.at[piece], nxs, nxr.at[sem], at(0, 0, to))
+
+    def pass_on(dx):
+        piece = pl.ds(((x + dx) % X) * xrows, xrows)
+        start(frow.at[piece], fpart.at[piece], ncs, ncr.at[dx], partner)
+
+    def landed(dx, half, sem):
+        wait_rows(frow, ((x + dx) % X) * xrows + half * hrows, hrows, nxr.at[sem])
+
+    wait_rows(frow, 0, (Z - 1) * yrows, nzr)
+    along(0, 0, 0, 1)
+    if X > 2:
+        along(0, 1, 2, X - 1)
+    along(0, 1, 1, 1)
+    if X > 2:
+        along(0, 0, 3, X - 1)
+    pass_on(0)
     xs = iota((128, own), 1) % (2 * X)
     lane_of = (xs // 2) * 8 + (xs % 2) * 2
     j = iota((128, own), 0)
@@ -270,31 +306,6 @@
         start(abuf.at[pl.ds(d * Z, Z)], ay.at[pl.ds(y * Z, Z)], ays, ayr, at(0, -d))
     ay[pl.ds(y * Z, Z), :] = abuf[0:Z, :]
 
-    xrows = nyz * half_t
-    hrows = xrows // 2
-
-    def block_of(dx, half):
-        return pl.ds(((x + dx) % X) * xrows + half * hrows, hrows)
-
-    def along(dx, half, sem, to):
-        piece = block_of(dx, half)
-        start(frow.at[piece], frow.at[piece], nxs, nxr.at[sem], at(0, 0, to))
-
-    def pass_on(dx):
-        piece = pl.ds(((x + dx) % X) * xrows, xrows)
-        start(frow.at[piece], fpart.at[piece], ncs, ncr.at[dx], partner)
-
-    def landed(dx, half, sem):
-        wait_rows(frow, ((x + dx) % X) * xrows + half * hrows, hrows, nxr.at[sem])
-
-    wait_rows(frow, 0, (Z - 1) * yrows, nzr)
-    along(0, 0, 0, 1)
-    if X > 2:
-        along(0, 1, 2, X - 1)
-    along(0, 1, 1, 1)
-    if X > 2:
-        along(0, 0, 3, X - 1)
-    pass_on(0)
     if X > 2:
         landed(X - 1, 0, 0)
         along(X - 1, 0, 4, 1)
@@ -327,14 +338,19 @@
     ans[pl.ds(x * 8, 8), :] = abuf[0:8, :]
 
     if X > 2:
-        landed(2, 0, 4)
-        landed(2, 1, 5)
-        pass_on(2)
+        for half in range(2):
+            landed(2, half, 4 + half)
+            piece = block_of(2, half)
+            start(frow.at[piece], fpart.at[piece], ncs, ncr.at[2 * (half + 1)], partner)
+        for half in range(2):
+            wait_rows(fpart, ((x + 2) % X) * xrows + half * hrows, hrows, ncr.at[2 * (half + 1)])
     for dx in range(X):
-        wait_rows(fpart, ((x + dx) % X) * xrows, xrows, ncr.at[dx])
+        if dx != 2:
+            wait_rows(fpart, ((x + dx) % X) * xrows, xrows, ncr.at[dx])
     wait_rows(ans, 0, (X - 1) * 8, axr)
 
-    wait_rows(send, 0, (chips - 1) * msg, fs)
+    wait_rows(send, 0, (X - 1) * nyz * msg, gs)
+    wait_rows(send, 0, (nyz - 1) * X * msg, fs)
     wait_rows(part_sum, 0, 1, ss)
     wait_rows(recv, 0, n_group * grows, ps)
     wait_rows(frow, 0, (Y - 1) * half_t, nys)
@@ -419,6 +435,8 @@
             pltpu.VMEM((rows, width), f32),
             pltpu.VMEM((1, rows), jnp.int32),
             pltpu.VMEM((linear, 128), f32),
+            pltpu.VMEM((linear // X * (X - 1), 128), f32),
+            pltpu.VMEM((linear, 128), f32),
             pltpu.VMEM((linear, 128), f32),
             pltpu.VMEM((linear, 128), f32),
             pltpu.VMEM((4 * chips + 16, width), bf16),
@@ -431,10 +449,10 @@
             pltpu.VMEM((nyz, 128), f32),
             pltpu.VMEM((nyz, 128), f32),
             pltpu.VMEM((nyz, 128), f32),
-            regular, regular,
-            dma((5,)),
+            regular,
+            dma((5,)), dma, dma((n_group,)),
             dma, dma((n_group,)), dma, dma((n_group,)), dma, dma,
-            dma, dma, dma, dma, dma, dma((6,)), dma, dma((X,)),
+            dma, dma, dma, dma, dma, dma((6,)), dma, dma((X + 1,)),
             dma, dma, dma, dma, dma, dma,
         ],
         compiler_params=pltpu.CompilerParams(

time: 81.4 us -> 81.7 us (level); the launches traced: 81 us -> 80.2 us
  no operation moved by 1% of the time
where the time goes in v8:
time: 81.7 us; the launch traced here: 80.2 us
  Pallas kernels  78.9 us (97%)
    pallas_call x1, Pallas kernels, local(): pl.pallas_call(functools.partial(exchange, dims), out_shape=(shape((half,...  77.5 us

profile of v8, /device:TPU:1, one launch (start us, length us, event | category | flops | bytes accessed | tf_op | source)
XLA Modules:
  0.0 80.2 jit_solution(14983514106175074569)
XLA Ops:
  0.6 0.0 copy-start.2
  0.6 0.0 copy-start.1
  0.7 0.7 copy-done.2
  1.3 0.0 copy-done.1
  1.3 0.0 copy-start
  1.3 77.5 %shard_map.67 = (f32[768,128]{1,0:T(8,128)S(1)}, f32[768,128]{1,0:T(8,128)S(1)}, f32[32,128]{1,0:T(8,128)S(1)}) custom-call(f32[256,768]{1,0:T(8,128)} %emb_hbm.1, s32[1,256]{1,0:T(1,128)S(1)} %bitcast.4, s32[1,256]{1,0:T(1,128)S(1)} %bitcast.6), custom_call_target="tpu_custom_call" | custom-call | tf_op jit(solution)/shard_map/pallas_call | solution.py:425
  78.9 0.0 copy-done
  78.9 1.3 %shard_map.68 = (f32[128,768]{1,0:T(8,128)}, f32[1,256]{1,0:T(1,128)}, f32[1,256]{1,0:T(1,128)}) custom-call(f32[768,128]{1,0:T(8,128)S(1)} %get-tuple-element.9.frow, f32[768,128]{1,0:T(8,128)S(1)} %get-tuple-element.10.fpart, f32[32,128]{1,0:T(8,128)S(1)} %get-tuple-element.11.ans, s32[1,256]{1,0:T(1,128)S(1)} %bitcast.5, s32[1,256]{1,0:T(1,128)S(1)} %bitcast.7, ...), custom_call_target="tpu_custom_call" | custom-call | tf_op jit(solution)/shard_map/pallas_call | solution.py:462
Async XLA Ops:
  0.6 0.7 copy-start.2
  0.6 0.7 copy-start.1
  1.3 77.6 %copy-start = (f32[128,768]{1,0:T(8,128)S(1)}, f32[128,768]{1,0:T(8,128)}, u32[]{:S(2)}) copy-start(f32[128,768]{1,0:T(8,128)} %cent.1) | copy-start | bytes 1179652

commit v9 on v7

--- a/solution.py
+++ b/solution.py
@@ -208,15 +208,12 @@
         wait_rows(recv, g * grows + missing, grows - missing, fr.at[g])
         piece = pl.ds(g * grows, grows)
         start(recv.at[piece], other.at[piece], ps, pr.at[g], partner)
-        if g > 0:
-            mine = take_own(g - 1, mine)
-        if g > 1:
-            take_other(g - 2)
-    mine = take_own(n_group - 1, mine)
+        mine = take_own(g, mine)
+        if g < n_group - 1:
+            take_other(g)
     part_sum[0] = mine
     start(part_sum.at[0], part_sum.at[1], ss, sr, partner)
-    for g in range(max(n_group - 2, 0), n_group):
-        take_other(g)
+    take_other(n_group - 1)
 
     wait_rows(part_sum, 1, 1, sr)
     sums = mine + part_sum[1]
@@ -295,18 +292,26 @@
     if X > 2:
         along(0, 0, 3, X - 1)
     pass_on(0)
-    if X > 2:
-        landed(X - 1, 0, 0)
-        along(X - 1, 0, 4, 1)
-        landed(1, 1, 2)
-        along(1, 1, 5, X - 1)
-
     wait_rows(ay, 0, (Y - 1) * Z, ayr)
     for dz in range(Z):
         ab[dz * Y:(dz + 1) * Y, :] = ay[pl.ds(dz, Y, stride=Z), :]
     for d in range(1, Z):
         start(ab.at[pl.ds(d * Y, Y)], az.at[pl.ds(z * Y, Y)], azs, azr, at(-d, 0))
     az[pl.ds(z * Y, Y), :] = ab[0:Y, :]
+
+    if X > 2:
+        landed(X - 1, 0, 0)
+        along(X - 1, 0, 4, 1)
+        landed(1, 1, 2)
+        along(1, 1, 5, X - 1)
+
+    wait_rows(az, 0, (Z - 1) * Y, azr)
+    wait_rows(ay, 0, (Y - 1) * Z, ays)
+    turned = jnp.concatenate([az[...], jnp.zeros((128 - nyz, 128), f32)], axis=0).T
+    abuf[0:8 * X, :] = turned[0:8 * X, :]
+    for d in range(1, X):
+        start(abuf.at[pl.ds(d * 8, 8)], ans.at[pl.ds(x * 8, 8)], axs, axr, at(0, 0, X - d))
+    ans[pl.ds(x * 8, 8), :] = abuf[0:8, :]
 
     if X > 2:
         landed(X - 1, 1, 1)
@@ -318,20 +323,16 @@
         landed(1, 1, 1)
         pass_on(1)
 
-    wait_rows(az, 0, (Z - 1) * Y, azr)
-    wait_rows(ay, 0, (Y - 1) * Z, ays)
-    turned = jnp.concatenate([az[...], jnp.zeros((128 - nyz, 128), f32)], axis=0).T
-    abuf[0:8 * X, :] = turned[0:8 * X, :]
-    for d in range(1, X):
-        start(abuf.at[pl.ds(d * 8, 8)], ans.at[pl.ds(x * 8, 8)], axs, axr, at(0, 0, X - d))
-    ans[pl.ds(x * 8, 8), :] = abuf[0:8, :]
-
     if X > 2:
-        landed(2, 0, 4)
-        landed(2, 1, 5)
-        pass_on(2)
+        for side in range(2):
+            landed(2, side, 4 + side)
+            piece = block_of(2, side)
+            start(frow.at[piece], fpart.at[piece], ncs, ncr.at[2 * (side + 1)], partner)
+        for side in range(2):
+            wait_rows(fpart, ((x + 2) % X) * xrows + side * hrows, hrows, ncr.at[2 * (side + 1)])
     for dx in range(X):
-        wait_rows(fpart, ((x + dx) % X) * xrows, xrows, ncr.at[dx])
+        if dx != 2:
+            wait_rows(fpart, ((x + dx) % X) * xrows, xrows, ncr.at[dx])
     wait_rows(ans, 0, (X - 1) * 8, axr)
 
     wait_rows(send, 0, (chips - 1) * msg, fs)
@@ -434,7 +435,7 @@
             regular, regular,
             dma((5,)),
             dma, dma((n_group,)), dma, dma((n_group,)), dma, dma,
-            dma, dma, dma, dma, dma, dma((6,)), dma, dma((X,)),
+            dma, dma, dma, dma, dma, dma((6,)), dma, dma((X + 1,)),
             dma, dma, dma, dma, dma, dma,
         ],
         compiler_params=pltpu.CompilerParams(

time: 81.4 us -> 79.5 us (0.977)
  Pallas kernels: 79.6 us -> 78.1 us
    pallas_call x1, Pallas kernels: 78.3 us -> 76.7 us  [local(): pl.pallas_call(functools.partial(exchange, dims), out_shape=(shape((half,...]
where the time goes in v9:
time: 79.5 us; the launch traced here: 79.4 us
  Pallas kernels  78.1 us (98%)
    pallas_call x1, Pallas kernels, local(): pl.pallas_call(functools.partial(exchange, dims), out_shape=(shape((half,...  76.7 us

profile of v9, /device:TPU:1, one launch (start us, length us, event | category | flops | bytes accessed | tf_op | source)
XLA Modules:
  0.0 79.4 jit_solution(6055890502987699824)
XLA Ops:
  0.6 0.0 copy-start.2
  0.6 0.0 copy-start.1
  0.7 0.7 copy-done.2
  1.3 0.0 copy-done.1
  1.3 0.0 copy-start
  1.3 76.7 %shard_map.67 = (f32[768,128]{1,0:T(8,128)S(1)}, f32[768,128]{1,0:T(8,128)S(1)}, f32[32,128]{1,0:T(8,128)S(1)}) custom-call(f32[256,768]{1,0:T(8,128)} %emb_hbm.1, s32[1,256]{1,0:T(1,128)S(1)} %bitcast.4, s32[1,256]{1,0:T(1,128)S(1)} %bitcast.6), custom_call_target="tpu_custom_call" | custom-call | tf_op jit(solution)/shard_map/pallas_call | solution.py:410
  78.1 0.0 copy-done
  78.1 1.3 %shard_map.68 = (f32[128,768]{1,0:T(8,128)}, f32[1,256]{1,0:T(1,128)}, f32[1,256]{1,0:T(1,128)}) custom-call(f32[768,128]{1,0:T(8,128)S(1)} %get-tuple-element.9.frow, f32[768,128]{1,0:T(8,128)S(1)} %get-tuple-element.10.fpart, f32[32,128]{1,0:T(8,128)S(1)} %get-tuple-element.11.ans, s32[1,256]{1,0:T(1,128)S(1)} %bitcast.5, s32[1,256]{1,0:T(1,128)S(1)} %bitcast.7, ...), custom_call_target="tpu_custom_call" | custom-call | tf_op jit(solution)/shard_map/pallas_call | solution.py:445
Async XLA Ops:
  0.6 0.7 copy-start.2
  0.6 0.7 copy-start.1
  1.3 76.7 %copy-start = (f32[128,768]{1,0:T(8,128)S(1)}, f32[128,768]{1,0:T(8,128)}, u32[]{:S(2)}) copy-start(f32[128,768]{1,0:T(8,128)} %cent.1) | copy-start | bytes 1179652
